TPU v7x, 512 devices: a whole 4x8x8 slice. The times are simulated.
512 devices in a mesh: rep: 32 (over x, z), outer: 8 (over y), tp: 2 (over core).
Axes of the slice: x: 4, y: 8, z: 8, core: 2. Of those that a mesh axis runs over, the one named last changes fastest.
Arguments:
- activations: bfloat16 [8, 32, 128, 8192], P('outer', 'rep'), may hold values from -6 to 6
- kv_grads: bfloat16 [8, 32, 128, 2048], P('outer', 'rep', None, 'tp'), may hold values from -0.119628906 to 0.119628906
- kept_blocks: int32 [8, 32, 2, 1024], P('outer', 'rep', 'tp'), may hold values from 0 to 65535, as said below
- region_bounds: int32 [33], replicated, may hold values from 0 to 65536, as said below
- region_keep: int32 [32, 256], P('rep'), may hold values from 0 to 2303, as said below
- residual: float32 [8, 32, 2304, 256], P('outer', 'rep', None, 'tp'), may hold values from -6 to 6
Outputs:
- merged: float32 [32, 256, 256], P('rep', 'outer', 'tp')
- new_residual: float32 [8, 32, 2304, 256], P('outer', 'rep', None, 'tp')
Inputs may be any that keep to these rules, and one draw needn't show every extreme that they name: `kept_blocks`: ids of one list are distinct. Of one replica's list for one column half, at most 64 fall in one region, exactly 64 in some region, and there is a region that receives exactly 64 from every replica and half. `region_bounds`: rising from 0 to 65536; every region holds 1792 to 2304 blocks, one exactly 2304. `region_keep`: distinct slots of each region, below the region's length.
All inputs are finite; a program needn't handle non-finite values.
Results may differ from a plain program's by a relative error of at most 0.002.
Values sent between devices are 32-bit elements; how exact they have to be, the bound alone decides.
No kernel may reach another device: no remote copies, remote signals or barrier semaphores. Data moves between devices by JAX's collectives and lax.ppermute only.
A program may use at most 128 MiB of HBM per device.

v0:
```python
import jax
import jax.numpy as jnp
from jax import lax
from jax.sharding import PartitionSpec as P

HEAD = 128
CAP = 64


def swapped(block, axis, apart):
    count = lax.axis_size(axis)
    route = []
    for low in range(count):
        high = low | 1 << apart
        if high != low and high < count:
            route += [(low, high), (high, low)]
    return lax.ppermute(block, axis, route)


def exact_parts(values):
    high_part = values.astype(jnp.bfloat16)
    rest = values - high_part.astype(jnp.float32)
    middle_part = rest.astype(jnp.bfloat16)
    low_part = (rest - middle_part.astype(jnp.float32)).astype(jnp.bfloat16)
    return (high_part, middle_part, low_part)


def body(activations, kv_grads, kept_blocks, region_bounds, region_keep, residual):
    inputs = activations[0, 0]
    grad_cols = kv_grads[0, 0]
    block_ids = kept_blocks[0, 0, 0]
    model_width = inputs.shape[1]
    column_blocks = grad_cols.shape[1] // HEAD
    keep_count = block_ids.shape[0]
    slot_count = residual.shape[2]
    region_count = lax.axis_size("rep")
    contract = (((0,), (0,)), ((), ()))
    row_span = min(model_width, 1024)
    values = jnp.zeros((keep_count, HEAD), jnp.float32)
    for row_first in range(0, model_width, row_span):
        partial_value = lax.dot_general(
            inputs[:, row_first : row_first + row_span],
            grad_cols,
            contract,
            preferred_element_type=jnp.float32,
        )
        blocks = partial_value.reshape(row_span * column_blocks, HEAD)
        local_ids = block_ids - row_first * column_blocks
        inside = (local_ids >= 0) & (local_ids < row_span * column_blocks)
        picked = jnp.take(blocks, jnp.clip(local_ids, 0, row_span * column_blocks - 1), axis=0)
        values = values + jnp.where(inside[:, None], picked, 0.0)
    region_starts = region_bounds[:region_count]
    owners = jnp.sum(
        (block_ids[:, None] >= region_bounds[None, 1:region_count]).astype(jnp.int32), axis=1
    )
    onehot = (owners[:, None] == jnp.arange(region_count, dtype=jnp.int32)[None, :]).astype(
        jnp.int32
    )
    ranking = jnp.sum((jnp.cumsum(onehot, axis=0) - onehot) * onehot, axis=1)
    offsets = block_ids - jnp.sum(onehot * region_starts[None, :], axis=1)
    destination = owners * CAP + ranking
    slot_index = jnp.arange(region_count * CAP, dtype=jnp.int32)
    matches = slot_index[:, None] == destination[None, :]
    source_row = (
        jnp.sum(jnp.where(matches, jnp.arange(keep_count, dtype=jnp.int32)[None, :] + 1, 0), axis=1)
        - 1
    )
    source_off = jnp.sum(jnp.where(matches, offsets[None, :] + 1, 0), axis=1) - 1
    filled = source_row >= 0
    send_vals = jnp.where(
        filled[:, None], jnp.take(values, jnp.maximum(source_row, 0), axis=0), 0.0
    ).reshape(region_count, CAP, HEAD)
    send_offs = source_off.reshape(region_count, CAP)
    got_vals, got_offs = (
        lax.all_to_all(send_vals, "rep", split_axis=0, concat_axis=0, tiled=True),
        lax.all_to_all(send_offs, "rep", split_axis=0, concat_axis=0, tiled=True),
    )
    flat_offs = got_offs.reshape(-1)
    placing = (jnp.arange(slot_count, dtype=jnp.int32)[:, None] == flat_offs[None, :]).astype(
        jnp.bfloat16
    )
    summed = jnp.zeros((slot_count, HEAD), jnp.float32)
    for piece in exact_parts(got_vals.reshape(-1, HEAD)):
        summed = summed + jnp.dot(placing, piece, preferred_element_type=jnp.float32)
    totals = summed + residual[0, 0]
    keep_slots = region_keep[0]
    chosen = jnp.take(totals, keep_slots, axis=0)
    share_rows = chosen.shape[0] // lax.axis_size("outer")
    for bit_pos in range(lax.axis_size("outer").bit_length() - 1):
        chosen = chosen + swapped(chosen, "outer", bit_pos)
    merged = lax.dynamic_slice_in_dim(chosen, lax.axis_index("outer") * share_rows, share_rows, 0)
    owner_index = lax.axis_index("rep")
    region_length = region_bounds[owner_index + 1] - region_bounds[owner_index]
    slot_ids = jnp.arange(slot_count, dtype=jnp.int32)
    named = jnp.any(slot_ids[:, None] == keep_slots[None, :], axis=1)
    survive = (slot_ids < region_length) & jnp.logical_not(named)
    refreshed = jnp.where(survive[:, None], totals, 0.0)
    return (merged[None], refreshed[None, None])


def solution(mesh):
    placed = (
        P("outer", "rep", None, None),
        P("outer", "rep", None, "tp"),
        P("outer", "rep", "tp", None),
        P(),
        P("rep", None),
        P("outer", "rep", None, "tp"),
    )
    return jax.shard_map(
        body,
        mesh=mesh,
        in_specs=placed,
        out_specs=(P("rep", "outer", "tp"), P("outer", "rep", None, "tp")),
        check_vma=False,
    )
```

profile of v0, /device:TPU:56, one launch (start us, length us, event | category | flops | bytes accessed | tf_op | source)
XLA Modules:
  0.0 228.3 jit_solution(6038002585692404596)
XLA Ops:
  0.7 0.9 slice.36
  1.5 0.8 convert_reduce_fusion
  2.3 9.0 %reduce-window.6 = s32[32,8,128]{2,1,0:T(8,128)S(1)} reduce-window(s32[32,8,128]{2,1,0:T(8,128)S(1)} %fusion.45, s32[]{:T(128)} %constant.43.clone.1), window={size=1x1x128 pad=0_0x0_0x127_0}, to_apply=%region_1.2 | reduce-window | flops 4161536 | bytes 262148 | tf_op jit(solution)/shard_map/reduce-window
  11.4 0.1 slice.68
  11.5 0.1 copy.10
  11.6 0.1 copy.11
  11.7 0.1 broadcast_add_fusion
  11.8 0.7 select_reduce_fusion.2
  12.6 0.7 subtract_add_fusion
  13.3 2.4 %select_reduce_fusion.1 = (s32[2048]{0:T(1024)S(1)}, s32[2048]{0:T(1024)S(1)}) fusion(s32[1024]{0:T(1024)S(1)} %get-tuple-element.11, s32[1024]{0:T(1024)S(1)} %get-tuple-element.38, s32[1024]{0:T(1024)S(1)} %iota_add_fusion), kind=kLoop, calls=%fused_computation.18 | loop fusion | flops 10481664 | bytes 28672 | tf_op jit(solution)/shard_map/reduce_sum | solution.py:68
  15.7 0.7 sub.60
  16.4 13.2 %all-to-all-start = ((s32[32,1,64]{2,1,0:T(1,128)}), s32[32,1,64]{2,1,0:T(1,128)S(1)}, u32[]{:S(2)}, u32[]{:S(2)}) async-start(s32[32,1,64]{2,1,0:T(1,128)} %sub.60), calls=%async_computation | async-start | bytes 32768 | tf_op jit(solution)/shard_map/all_to_all | solution.py:76
  29.6 3.6 %fusion.32 = f32[1024,1024]{1,0:T(8,128)} fusion(bf16[128,8192]{1,0:T(8,128)(2,1)} %bitcast.68, bf16[1,1,128,1024]{3,2,1,0:T(8,128)(2,1)S(1)} %copy-done), kind=kOutput, calls=%fused_computation.60 | convolution fusion | flops 268435456 | bytes 4718592 | tf_op jit(solution)/shard_map/dot_general | solution.py:41
  33.2 2.7 %fusion.30 = f32[1024,1024]{1,0:T(8,128)} fusion(bf16[128,8192]{1,0:T(8,128)(2,1)S(1)} %bitcast.69, bf16[1,1,128,1024]{3,2,1,0:T(8,128)(2,1)S(1)} %copy-done), kind=kOutput, calls=%fused_computation.58 | convolution fusion | flops 268435456 | bytes 4718592 | tf_op jit(solution)/shard_map/dot_general | solution.py:41
  35.9 2.7 %fusion.28 = f32[1024,1024]{1,0:T(8,128)} fusion(bf16[128,8192]{1,0:T(8,128)(2,1)S(1)} %bitcast.70, bf16[1,1,128,1024]{3,2,1,0:T(8,128)(2,1)S(1)} %copy-done), kind=kOutput, calls=%fused_computation.56 | convolution fusion | flops 268435456 | bytes 4718592 | tf_op jit(solution)/shard_map/dot_general | solution.py:41
  38.6 2.8 %fusion.26 = f32[1024,1024]{1,0:T(8,128)} fusion(bf16[128,8192]{1,0:T(8,128)(2,1)S(1)} %bitcast.71, bf16[1,1,128,1024]{3,2,1,0:T(8,128)(2,1)S(1)} %copy-done), kind=kOutput, calls=%fused_computation.54 | convolution fusion | flops 268435456 | bytes 4718592 | tf_op jit(solution)/shard_map/dot_general | solution.py:41
  41.4 2.7 %fusion.24 = f32[1024,1024]{1,0:T(8,128)} fusion(bf16[128,8192]{1,0:T(8,128)(2,1)S(1)} %bitcast.72, bf16[1,1,128,1024]{3,2,1,0:T(8,128)(2,1)S(1)} %copy-done), kind=kOutput, calls=%fused_computation.52 | convolution fusion | flops 268435456 | bytes 4718592 | tf_op jit(solution)/shard_map/dot_general | solution.py:41
  44.1 2.7 %fusion.22 = f32[1024,1024]{1,0:T(8,128)} fusion(bf16[128,8192]{1,0:T(8,128)(2,1)S(1)} %bitcast.73, bf16[1,1,128,1024]{3,2,1,0:T(8,128)(2,1)S(1)} %copy-done), kind=kOutput, calls=%fused_computation.50 | convolution fusion | flops 268435456 | bytes 4718592 | tf_op jit(solution)/shard_map/dot_general | solution.py:41
  46.7 2.7 %fusion.20 = f32[1024,1024]{1,0:T(8,128)} fusion(bf16[128,8192]{1,0:T(8,128)(2,1)S(1)} %bitcast.74, bf16[1,1,128,1024]{3,2,1,0:T(8,128)(2,1)S(1)} %copy-done), kind=kOutput, calls=%fused_computation.48 | convolution fusion | flops 268435456 | bytes 4718592 | tf_op jit(solution)/shard_map/dot_general | solution.py:41
  49.4 2.7 %fusion.18 = f32[1024,1024]{1,0:T(8,128)} fusion(bf16[128,8192]{1,0:T(8,128)(2,1)S(1)} %bitcast.75, bf16[1,1,128,1024]{3,2,1,0:T(8,128)(2,1)S(1)} %copy-done), kind=kOutput, calls=%fused_computation.46 | convolution fusion | flops 268435456 | bytes 4718592 | tf_op jit(solution)/shard_map/dot_general | solution.py:41
  52.2 4.9 %reshape.246 = f32[8192,128]{1,0:T(8,128)} reshape(f32[1024,1024]{1,0:T(8,128)} %fusion.32) | data formatting | bytes 8388608 | tf_op jit(solution)/shard_map/reshape | solution.py:47
  57.1 4.9 %reshape.247 = f32[8192,128]{1,0:T(8,128)} reshape(f32[1024,1024]{1,0:T(8,128)} %fusion.30) | data formatting | bytes 8388608 | tf_op jit(solution)/shard_map/reshape | solution.py:47
  62.0 4.9 %reshape.248 = f32[8192,128]{1,0:T(8,128)} reshape(f32[1024,1024]{1,0:T(8,128)} %fusion.28) | data formatting | bytes 8388608 | tf_op jit(solution)/shard_map/reshape | solution.py:47
  66.9 4.9 %reshape.249 = f32[8192,128]{1,0:T(8,128)} reshape(f32[1024,1024]{1,0:T(8,128)} %fusion.26) | data formatting | bytes 8388608 | tf_op jit(solution)/shard_map/reshape | solution.py:47
  71.8 4.9 %reshape.250 = f32[8192,128]{1,0:T(8,128)} reshape(f32[1024,1024]{1,0:T(8,128)} %fusion.24) | data formatting | bytes 8388608 | tf_op jit(solution)/shard_map/reshape | solution.py:47
  76.7 4.9 %reshape.251 = f32[8192,128]{1,0:T(8,128)} reshape(f32[1024,1024]{1,0:T(8,128)} %fusion.22) | data formatting | bytes 8388608 | tf_op jit(solution)/shard_map/reshape | solution.py:47
  81.6 4.9 %reshape.252 = f32[8192,128]{1,0:T(8,128)} reshape(f32[1024,1024]{1,0:T(8,128)} %fusion.20) | data formatting | bytes 8388608 | tf_op jit(solution)/shard_map/reshape | solution.py:47
  86.5 4.9 %reshape.253 = f32[8192,128]{1,0:T(8,128)} reshape(f32[1024,1024]{1,0:T(8,128)} %fusion.18) | data formatting | bytes 8388608 | tf_op jit(solution)/shard_map/reshape | solution.py:47
  91.4 0.1 ge.108
  91.4 0.1 le.37
  91.5 5.0 %gather_fusion.2 = f32[1024,128]{1,0:T(8,128)S(1)} fusion(f32[8192,128]{1,0:T(8,128)} %reshape.246, s32[1024]{0:T(1024)S(1)} %get-tuple-element.18), kind=kCustom, calls=%fused_computation.clone | custom fusion | bytes 1052672 | tf_op jit(solution)/shard_map/jit(_take)/gather | solution.py:50
  96.5 5.0 %gather_fusion.3 = f32[1024,128]{1,0:T(8,128)S(1)} fusion(f32[8192,128]{1,0:T(8,128)} %reshape.247, s32[1024]{0:T(1024)S(1)} %get-tuple-element.17), kind=kCustom, calls=%fused_computation.1.clone | custom fusion | bytes 1052672 | tf_op jit(solution)/shard_map/jit(_take)/gather | solution.py:50
  101.5 5.0 %gather_fusion.4 = f32[1024,128]{1,0:T(8,128)S(1)} fusion(f32[8192,128]{1,0:T(8,128)} %reshape.248, s32[1024]{0:T(1024)S(1)} %get-tuple-element.16), kind=kCustom, calls=%fused_computation.2.clone | custom fusion | bytes 1052672 | tf_op jit(solution)/shard_map/jit(_take)/gather | solution.py:50
  106.5 5.0 %gather_fusion.5 = f32[1024,128]{1,0:T(8,128)S(1)} fusion(f32[8192,128]{1,0:T(8,128)} %reshape.249, s32[1024]{0:T(1024)S(1)} %get-tuple-element.15), kind=kCustom, calls=%fused_computation.3.clone | custom fusion | bytes 1052672 | tf_op jit(solution)/shard_map/jit(_take)/gather | solution.py:50
  111.5 5.0 %gather_fusion.6 = f32[1024,128]{1,0:T(8,128)S(1)} fusion(f32[8192,128]{1,0:T(8,128)} %reshape.250, s32[1024]{0:T(1024)S(1)} %get-tuple-element.14), kind=kCustom, calls=%fused_computation.4.clone | custom fusion | bytes 1052672 | tf_op jit(solution)/shard_map/jit(_take)/gather | solution.py:50
  116.5 6.2 %gather_fusion.7 = f32[1024,128]{1,0:T(8,128)} fusion(f32[8192,128]{1,0:T(8,128)} %reshape.251, s32[1024]{0:T(1024)S(1)} %get-tuple-element.13), kind=kCustom, calls=%fused_computation.5.clone | custom fusion | bytes 1052672 | tf_op jit(solution)/shard_map/jit(_take)/gather | solution.py:50
  122.7 6.2 %gather_fusion.8 = f32[1024,128]{1,0:T(8,128)} fusion(f32[8192,128]{1,0:T(8,128)} %reshape.252, s32[1024]{0:T(1024)S(1)} %get-tuple-element.12), kind=kCustom, calls=%fused_computation.6.clone | custom fusion | bytes 1052672 | tf_op jit(solution)/shard_map/jit(_take)/gather | solution.py:50
  128.9 6.2 %gather_fusion.9 = f32[1024,128]{1,0:T(8,128)} fusion(f32[8192,128]{1,0:T(8,128)} %reshape.253, s32[1024]{0:T(1024)S(1)} %get-tuple-element.19), kind=kCustom, calls=%fused_computation.7.clone | custom fusion | bytes 1052672 | tf_op jit(solution)/shard_map/jit(_take)/gather | solution.py:50
  135.1 5.5 %fusion.11 = f32[1024,128]{1,0:T(8,128)S(1)} fusion(f32[1024,128]{1,0:T(8,128)} %gather_fusion.9, f32[1024,128]{1,0:T(8,128)} %gather_fusion.8, f32[1024,128]{1,0:T(8,128)} %gather_fusion.7, f32[1024,128]{1,0:T(8,128)S(1)} %gather_fusion.6, f32[1024,128]{1,0:T(8,128)S(1)} %gather_fusion.5, f32[1024,128]{1,0:T(8,128)S(1)} %gather_fusion.4, ...), kind=kLoop, calls=%fused_computation.32 | loop fusion | flops 3014656 | bytes 4734976 | tf_op jit(solution)/shard_map/add | solution.py:51
  140.6 5.5 %gather_fusion = f32[2048,128]{1,0:T(8,128)S(1)} fusion(f32[1024,128]{1,0:T(8,128)S(1)} %fusion.11, s32[2048]{0:T(1024)S(1)} %maximum_clamp_fusion), kind=kCustom, calls=%fused_computation.8 | custom fusion | bytes 2105344 | tf_op jit(solution)/shard_map/jit(_take)/gather | solution.py:71
  146.1 1.5 select_select_fusion
  147.6 10.0 %all-to-all-start.1 = ((f32[32,64,128]{2,1,0:T(8,128)}), f32[32,64,128]{2,1,0:T(8,128)S(1)}, u32[]{:S(2)}, u32[]{:S(2)}) async-start(f32[32,64,128]{2,1,0:T(8,128)} %select_select_fusion), calls=%async_computation.1 | async-start | bytes 2097152 | tf_op jit(solution)/shard_map/all_to_all | solution.py:75
  157.6 0.7 fusion.56
  159.7 0.5 broadcast.394
  160.2 0.7 reduce.3
  160.9 0.1 eq.75
  161.0 24.9 %all-to-all-done.1 = f32[32,64,128]{2,1,0:T(8,128)S(1)} async-done(((f32[32,64,128]{2,1,0:T(8,128)}), f32[32,64,128]{2,1,0:T(8,128)S(1)}, u32[]{:S(2)}, u32[]{:S(2)}) %all-to-all-start.1) | async-done | bytes 1048608 | tf_op jit(solution)/shard_map/all_to_all | solution.py:75
  185.9 0.2 subtract_convert_fusion
  186.1 3.4 %fusion.1 = f32[2304,128]{1,0:T(8,128)S(1)} fusion(bf16[2048,128]{1,0:T(8,128)(2,1)S(1)} %get-tuple-element.8, s32[2048]{0:T(1024)S(1)} %eq.75), kind=kOutput, calls=%fused_computation.12 | convolution fusion | flops 1212678144 | bytes 1712128 | tf_op jit(solution)/shard_map/dot_general | solution.py:84
  189.4 0.1 bitcast_convert_fusion
  189.5 3.3 %fusion.6 = f32[2304,128]{1,0:T(8,128)S(1)} fusion(f32[2304,128]{1,0:T(8,128)S(1)} %fusion.1, bf16[2048,128]{1,0:T(8,128)(2,1)S(1)} %bitcast_convert_fusion, s32[2048]{0:T(1024)S(1)} %eq.75), kind=kOutput, calls=%fused_computation.20 | convolution fusion | flops 1212973056 | bytes 2891776 | tf_op jit(solution)/shard_map/dot_general | solution.py:84
  192.9 3.4 %fusion.8 = f32[2304,128]{1,0:T(8,128)S(1)} fusion(f32[2304,128]{1,0:T(8,128)S(1)} %fusion.6, bf16[2048,128]{1,0:T(8,128)(2,1)S(1)} %get-tuple-element.7, s32[2048]{0:T(1024)S(1)} %eq.75, f32[1,1,2304,128]{3,2,1,0:T(8,128)S(1)} %copy-done.6), kind=kOutput, calls=%fused_computation.22 | convolution fusion | flops 1213267968 | bytes 4071424 | tf_op jit(solution)/shard_map/dot_general | solution.py:84
  196.2 0.7 gather_fusion.1
  197.0 0.1 broadcast_select_fusion
  197.1 3.3 %collective-permute-start = (f32[256,128]{1,0:T(8,128)S(1)}, f32[256,128]{1,0:T(8,128)S(1)}, u32[]{:S(2)}, u32[]{:S(2)}) collective-permute-start(f32[256,128]{1,0:T(8,128)S(1)} %broadcast_select_fusion), channel_id=1, source_target_pairs={{0,2},{2,0},{4,6},{6,4},{8,10},{10,8},{12,14},{14,12},{1,3},{3,1},... | collective-permute-start | bytes 393224 | tf_op jit(solution)/shard_map/ppermute | solution.py:17
  200.3 0.4 fusion.9
  200.7 4.1 %collective-permute-done = f32[256,128]{1,0:T(8,128)S(1)} collective-permute-done((f32[256,128]{1,0:T(8,128)S(1)}, f32[256,128]{1,0:T(8,128)S(1)}, u32[]{:S(2)}, u32[]{:S(2)}) %collective-permute-start) | collective-permute-done | bytes 131104 | tf_op jit(solution)/shard_map/ppermute | solution.py:17
  204.9 0.1 fusion.60
  205.0 4.3 %collective-permute-start.1 = (f32[256,128]{1,0:T(8,128)S(1)}, f32[256,128]{1,0:T(8,128)S(1)}, u32[]{:S(2)}, u32[]{:S(2)}) collective-permute-start(f32[256,128]{1,0:T(8,128)S(1)} %fusion.60), channel_id=1, source_target_pairs={{0,4},{4,0},{2,6},{6,2},{8,12},{12,8},{10,14},{14,10},{1,5},{5,1},... | collective-permute-start | bytes 393224 | tf_op jit(solution)/shard_map/ppermute | solution.py:17
  209.3 7.7 %collective-permute-done.1 = f32[256,128]{1,0:T(8,128)S(1)} collective-permute-done((f32[256,128]{1,0:T(8,128)S(1)}, f32[256,128]{1,0:T(8,128)S(1)}, u32[]{:S(2)}, u32[]{:S(2)}) %collective-permute-start.1) | collective-permute-done | bytes 131104 | tf_op jit(solution)/shard_map/ppermute | solution.py:17
  217.0 1.9 collective-permute-start.2
  218.9 2.1 select_bitcast_fusion
  220.9 6.8 %collective-permute-done.2 = f32[256,128]{1,0:T(8,128)S(1)} collective-permute-done((f32[256,128]{1,0:T(8,128)S(1)}, f32[256,128]{1,0:T(8,128)S(1)}, u32[]{:S(2)}, u32[]{:S(2)}) %collective-permute-start.2) | collective-permute-done | bytes 131104 | tf_op jit(solution)/shard_map/ppermute | solution.py:17
  227.7 0.6 fusion.46
  (28 shorter events, 0.2 us)
Async XLA Ops:
  0.6 28.9 %copy-start = (bf16[1,1,128,1024]{3,2,1,0:T(8,128)(2,1)S(1)}, bf16[1,1,128,1024]{3,2,1,0:T(8,128)(2,1)}, u32[]{:S(2)}) copy-start(bf16[1,1,128,1024]{3,2,1,0:T(8,128)(2,1)} %param.9) | copy-start | bytes 786436
  0.6 32.6 %copy-start.2 = (bf16[1,1,128,8192]{3,2,1,0:T(8,128)(2,1)S(1)}, bf16[1,1,128,8192]{3,2,1,0:T(8,128)(2,1)}, u32[]{:S(2)}) copy-start(bf16[1,1,128,8192]{3,2,1,0:T(8,128)(2,1)} %param.8) | copy-start | bytes 6291460
  16.4 131.3 %all-to-all-start = ((s32[32,1,64]{2,1,0:T(1,128)}), s32[32,1,64]{2,1,0:T(1,128)S(1)}, u32[]{:S(2)}, u32[]{:S(2)}) async-start(s32[32,1,64]{2,1,0:T(1,128)} %sub.60), calls=%async_computation | async-start | bytes 32768 | tf_op jit(solution)/shard_map/all_to_all | solution.py:76
  46.7 5.4 %copy-start.3 = (s32[1,1,1,1024]{3,2,1,0:T(1,128)S(1)}, s32[1,1,1,1024]{3,2,1,0:T(1,128)}, u32[]{:S(2)}) copy-start(s32[1,1,1,1024]{3,2,1,0:T(1,128)} %param.10) | copy-start | bytes 12292
  146.1 11.5 %copy-start.4 = (s32[33]{0:T(128)S(1)}, s32[33]{0:T(128)}, u32[]{:S(2)}) copy-start(s32[33]{0:T(128)} %param.11) | copy-start | bytes 400
  146.1 13.5 %copy-start.5 = (s32[1,256]{1,0:T(1,128)S(1)}, s32[1,256]{1,0:T(1,128)}, u32[]{:S(2)}) copy-start(s32[1,256]{1,0:T(1,128)} %param.12) | copy-start | bytes 3076
  147.6 38.2 %all-to-all-start.1 = ((f32[32,64,128]{2,1,0:T(8,128)}), f32[32,64,128]{2,1,0:T(8,128)S(1)}, u32[]{:S(2)}, u32[]{:S(2)}) async-start(f32[32,64,128]{2,1,0:T(8,128)} %select_select_fusion), calls=%async_computation.1 | async-start | bytes 2097152 | tf_op jit(solution)/shard_map/all_to_all | solution.py:75
  189.5 3.4 %copy-start.6 = (f32[1,1,2304,128]{3,2,1,0:T(8,128)S(1)}, f32[1,1,2304,128]{3,2,1,0:T(8,128)}, u32[]{:S(2)}) copy-start(f32[1,1,2304,128]{3,2,1,0:T(8,128)} %param.13) | copy-start | bytes 3538948
  192.9 35.5 %copy-start.1 = (bf16[1,1,128,1024]{3,2,1,0:T(8,128)(2,1)S(1)}, bf16[1,1,128,1024]{3,2,1,0:T(8,128)(2,1)}, u32[]{:S(2)}) copy-start(bf16[1,1,128,1024]{3,2,1,0:T(8,128)(2,1)} %param.9) | copy-start | bytes 786436
  197.1 7.8 %collective-permute-start = (f32[256,128]{1,0:T(8,128)S(1)}, f32[256,128]{1,0:T(8,128)S(1)}, u32[]{:S(2)}, u32[]{:S(2)}) collective-permute-start(f32[256,128]{1,0:T(8,128)S(1)} %broadcast_select_fusion), channel_id=1, source_target_pairs={{0,2},{2,0},{4,6},{6,4},{8,10},{10,8},{12,14},{14,12},{1,3},{3,1},... | collective-permute-start | bytes 393224 | tf_op jit(solution)/shard_map/ppermute | solution.py:17
  205.0 12.0 %collective-permute-start.1 = (f32[256,128]{1,0:T(8,128)S(1)}, f32[256,128]{1,0:T(8,128)S(1)}, u32[]{:S(2)}, u32[]{:S(2)}) collective-permute-start(f32[256,128]{1,0:T(8,128)S(1)} %fusion.60), channel_id=1, source_target_pairs={{0,4},{4,0},{2,6},{6,2},{8,12},{12,8},{10,14},{14,10},{1,5},{5,1},... | collective-permute-start | bytes 393224 | tf_op jit(solution)/shard_map/ppermute | solution.py:17
  217.0 10.8 %collective-permute-start.2 = (f32[256,128]{1,0:T(8,128)S(1)}, f32[256,128]{1,0:T(8,128)S(1)}, u32[]{:S(2)}, u32[]{:S(2)}) collective-permute-start(f32[256,128]{1,0:T(8,128)S(1)} %add.186), channel_id=1, source_target_pairs={{0,8},{8,0},{2,10},{10,2},{4,12},{12,4},{6,14},{14,6},{1,9},{9,1},... | collective-permute-start | bytes 393224 | tf_op jit(solution)/shard_map/ppermute | solution.py:17
where the time goes:
time: 230 us; the launch traced here: 228 us
  local copies, waits for them, and re-layouts  92.3 us (40%)
  waiting for transfers between devices  43.5 us (19%)
  starting transfers between devices  32.6 us (14%)
  matrix products  32.6 us (14%)
  other arithmetic  25.1 us (11%)
  between operations  2.33 us (1%)
    gather x8, local copies, waits for them, and re-layouts, body(): jnp.take(blocks, jnp.clip(local_ids, 0, row_span * column_blocks - 1), ax...  43.5 us
    reshape x8, local copies, waits for them, and re-layouts, body(): blocks = partial_value.reshape(row_span * column_blocks, HEAD)  39.2 us
    all_to_all x1, waiting for transfers between devices, body(): lax.all_to_all(send_vals, 'rep', split_axis=0, concat_axis=0, tiled=True)  24.9 us
    dot_general x8, matrix products, body(): lax.dot_general(inputs[:, row_first:row_first + row_span], grad_cols, con...  22.5 us
    ppermute x3, waiting for transfers between devices, swapped(): return lax.ppermute(block, axis, route)  18.6 us
    all_to_all x1, starting transfers between devices, body(): lax.all_to_all(send_offs, 'rep', split_axis=0, concat_axis=0, tiled=True)  13.2 us
    dot_general x3, matrix products, body(): jnp.dot(placing, piece, preferred_element_type=jnp.float32)  10.1 us
    all_to_all x1, starting transfers between devices, body(): lax.all_to_all(send_vals, 'rep', split_axis=0, concat_axis=0, tiled=True)  9.97 us
  transfers between devices with their start and end apart: 5, of which 4 were waited for; matrix products, arithmetic and copies ran while one was open for 54% of the time, Pallas kernels for 0%

commit v1 on v0

v1 whole, which is shorter than its diff:
```python
import functools

import jax
import jax.numpy as jnp
from jax import lax
from jax.experimental import pallas as pl
from jax.experimental.pallas import tpu as pltpu
from jax.sharding import PartitionSpec as P

HEAD = 128
CAP = 64
LANES = 128
SLOT_TILE = 256
MIB = 1 << 20
CONTRACT_LAST = (((1,), (1,)), ((), ()))


def contract_last(left, right):
    return lax.dot_general(left, right, CONTRACT_LAST, preferred_element_type=jnp.float32)


def send_kernel(band, batch, bounds_ref, ids_ref, act_ref, grad_ref, out_ref):
    regions = bounds_ref.shape[0] - 1
    keep_count = ids_ref.shape[1]
    width = act_ref.shape[1]
    column_blocks = grad_ref.shape[1] // HEAD
    column_bits = column_blocks.bit_length() - 1
    chunks = keep_count // LANES
    stride = CAP + 1

    region_row = lax.broadcasted_iota(jnp.int32, (regions, LANES), 0)
    starts = jnp.zeros((regions, LANES), jnp.int32)
    ends = jnp.zeros((regions, LANES), jnp.int32)
    for region in range(regions):
        starts = jnp.where(region_row == region, bounds_ref[region], starts)
        ends = jnp.where(region_row == region, bounds_ref[region + 1], ends)

    ids = [ids_ref[:, c * LANES : (c + 1) * LANES] for c in range(chunks)]
    owned = [(i >= starts) & (i < ends) for i in ids]
    owned_f = [jnp.where(o, 1.0, 0.0) for o in owned]
    stacked = jnp.concatenate(owned_f, axis=0).astype(jnp.bfloat16)
    before = lax.broadcasted_iota(jnp.int32, (LANES, 2 * LANES), 0)
    after = lax.broadcasted_iota(jnp.int32, (LANES, 2 * LANES), 1)
    ladder = jnp.where((before < after) | (after >= LANES), 1.0, 0.0).astype(jnp.bfloat16)
    counted = jnp.dot(stacked, ladder, preferred_element_type=jnp.float32)
    running = jnp.zeros((regions, LANES), jnp.float32)
    rank_row = lax.broadcasted_iota(jnp.int32, (2 * CAP, LANES), 0) & (CAP - 1)
    ranked, high_part, low_part = [], [], []
    for c in range(chunks):
        rows = slice(c * regions, (c + 1) * regions)
        here = counted[rows, :LANES] + running
        running = running + counted[rows, LANES:]
        rank = jnp.sum(owned_f[c] * here, axis=0, keepdims=True).astype(jnp.int32)
        ranked.append(jnp.where(rank_row == rank, 1.0, 0.0).astype(jnp.bfloat16))
        code = ids[c] + 1
        high_part.append((owned_f[c] * (code >> 8).astype(jnp.float32)).astype(jnp.bfloat16))
        low_part.append((owned_f[c] * (code & 255).astype(jnp.float32)).astype(jnp.bfloat16))
    ranked = jnp.concatenate(ranked, axis=1)
    high_part = jnp.concatenate(high_part, axis=1)
    low_part = jnp.concatenate(low_part, axis=1)
    by_region = 256.0 * contract_last(high_part, ranked) + contract_last(low_part, ranked) - 1.0
    ranked = ranked[:CAP]
    by_rank = 256.0 * contract_last(ranked, high_part) + contract_last(ranked, low_part) - 1.0
    offsets = jnp.where(by_region < 0.0, -1.0, by_region - starts.astype(jnp.float32))

    lane = lax.broadcasted_iota(jnp.int32, (CAP, LANES), 1)
    grads = grad_ref[...]
    for first in range(0, regions, batch):
        columns, picked = [], []
        for region in range(first, first + batch):
            wanted = jnp.broadcast_to(by_rank[:, region : region + 1], (CAP, LANES)).astype(jnp.int32)
            base = (bounds_ref[region] >> column_bits) & ~(LANES - 1)
            base = pl.multiple_of(jnp.minimum(base, width - band), LANES)
            place = (wanted >> column_bits) - base
            columns.append(wanted & (column_blocks - 1))
            chosen = jnp.concatenate(
                [
                    jnp.where(lane + part == place, 1.0, 0.0).astype(jnp.bfloat16)
                    for part in range(0, band, LANES)
                ],
                axis=1,
            )
            picked.append(contract_last(chosen, act_ref[:, pl.ds(base, band)]).astype(jnp.bfloat16))
        columns = jnp.concatenate(columns, axis=0)
        wide = jnp.dot(jnp.concatenate(picked, axis=0), grads, preferred_element_type=jnp.float32)
        block = wide[:, :HEAD]
        for column in range(1, column_blocks):
            block = jnp.where(columns == column, wide[:, column * HEAD : (column + 1) * HEAD], block)
        for step in range(batch):
            region = first + step
            out_ref[region * stride : region * stride + CAP, :] = block[step * CAP : (step + 1) * CAP]
            out_ref[region * stride + CAP : (region + 1) * stride, :] = offsets[region : region + 1]


def send_rows(region_bounds, block_ids, inputs, grad_cols, band):
    regions = region_bounds.shape[0] - 1
    vmem = pl.BlockSpec(memory_space=pltpu.VMEM)
    return pl.pallas_call(
        functools.partial(send_kernel, band, 4),
        out_shape=jax.ShapeDtypeStruct((regions * (CAP + 1), HEAD), jnp.float32),
        in_specs=[pl.BlockSpec(memory_space=pltpu.SMEM), vmem, vmem, vmem],
        out_specs=vmem,
        compiler_params=pltpu.CompilerParams(vmem_limit_bytes=24 * MIB),
        cost_estimate=pl.CostEstimate(flops=10**9, bytes_accessed=4 * MIB, transcendentals=0),
        name="send_rows",
    )(region_bounds, block_ids, inputs, grad_cols)


def keep_kernel(slots_ref, keep_ref, residual_ref, column_ref, rows_ref):
    count = keep_ref.shape[1]
    row = lax.broadcasted_iota(jnp.int32, (count, count), 0)
    lane = lax.broadcasted_iota(jnp.int32, (count, count), 1)
    spread = jnp.where(row == lane, jnp.broadcast_to(keep_ref[...], (count, count)), 0)
    column = jnp.sum(spread.astype(jnp.float32), axis=1, keepdims=True)
    column_ref[...] = jnp.broadcast_to(column, column_ref.shape)

    def step(first, carry):
        for inner in range(8):
            index = first * 8 + inner
            rows_ref[pl.ds(index, 1), :] = residual_ref[pl.ds(slots_ref[0, index], 1), :]
        return carry

    lax.fori_loop(0, count // 8, step, 0)


def kept_part(region_keep, residual):
    count = region_keep.shape[1]
    vmem = pl.BlockSpec(memory_space=pltpu.VMEM)
    return pl.pallas_call(
        keep_kernel,
        out_shape=[jax.ShapeDtypeStruct((count, HEAD), jnp.float32)] * 2,
        in_specs=[pl.BlockSpec(memory_space=pltpu.SMEM), vmem, vmem],
        out_specs=[vmem, vmem],
        compiler_params=pltpu.CompilerParams(vmem_limit_bytes=8 * MIB),
        cost_estimate=pl.CostEstimate(flops=10**8, bytes_accessed=4 * MIB, transcendentals=0),
        name="kept_part",
    )(region_keep, region_keep, residual)


def chosen_kernel(got_ref, column_ref, rows_ref, chosen_ref, parts_ref, offs_ref):
    sources = got_ref.shape[0] // (CAP + 1)
    stride = CAP + 1
    column = column_ref[...]
    lane = lax.broadcasted_iota(jnp.int32, (1, LANES), 1)
    places = []
    for pair in range(sources // 2):
        first = 2 * pair * stride + CAP
        offs = jnp.where(lane < CAP, got_ref[first : first + 1], got_ref[first + stride : first + stride + 1])
        offs_ref[:, pair * LANES : (pair + 1) * LANES] = offs
        places.append(jnp.where(column == offs, 1.0, 0.0).astype(jnp.bfloat16))
    for source in range(sources):
        values = got_ref[source * stride : source * stride + CAP]
        high = values.astype(jnp.bfloat16)
        low = (values - high.astype(jnp.float32)).astype(jnp.bfloat16)
        parts_ref[source * CAP : (source + 1) * CAP, :HEAD] = high
        parts_ref[source * CAP : (source + 1) * CAP, HEAD:] = low
    summed = jnp.dot(jnp.concatenate(places, axis=1), parts_ref[...], preferred_element_type=jnp.float32)
    chosen_ref[...] = summed[:, :HEAD] + summed[:, HEAD:] + rows_ref[...]


def chosen_totals(got, column, rows):
    sources = got.shape[0] // (CAP + 1)
    vmem = pl.BlockSpec(memory_space=pltpu.VMEM)
    return pl.pallas_call(
        chosen_kernel,
        out_shape=[
            jax.ShapeDtypeStruct(rows.shape, jnp.float32),
            jax.ShapeDtypeStruct((sources * CAP, 2 * HEAD), jnp.bfloat16),
            jax.ShapeDtypeStruct((1, sources * CAP), jnp.float32),
        ],
        in_specs=[vmem] * 3,
        out_specs=[vmem] * 3,
        compiler_params=pltpu.CompilerParams(vmem_limit_bytes=16 * MIB),
        cost_estimate=pl.CostEstimate(flops=10**8, bytes_accessed=4 * MIB, transcendentals=0),
        name="chosen_totals",
    )(got, column, rows)


def refresh_kernel(length_ref, offs_ref, parts_ref, keep_ref, residual_ref, out_ref):
    rows = out_ref.shape[0]
    base = pl.program_id(0) * rows
    length = length_ref[0]
    parts = parts_ref[...]
    keep = keep_ref[...]
    for first in range(0, rows, SLOT_TILE):
        slot = lax.broadcasted_iota(jnp.int32, (SLOT_TILE, LANES), 0) + (base + first)
        slot_f = slot.astype(jnp.float32)
        place = jnp.concatenate(
            [
                jnp.where(slot_f == offs_ref[:, part : part + LANES], 1.0, 0.0).astype(jnp.bfloat16)
                for part in range(0, offs_ref.shape[1], LANES)
            ],
            axis=1,
        )
        summed = jnp.dot(place, parts, preferred_element_type=jnp.float32)
        hits = jnp.zeros((SLOT_TILE, LANES), jnp.float32)
        for part in range(0, keep.shape[1], LANES):
            hits = hits + jnp.where(slot == keep[:, part : part + LANES], 1.0, 0.0)
        named = jnp.sum(hits, axis=1, keepdims=True)
        survive = (slot < length) & (jnp.broadcast_to(named, slot.shape) == 0.0)
        totals = summed[:, :HEAD] + summed[:, HEAD:] + residual_ref[first : first + SLOT_TILE]
        out_ref[first : first + SLOT_TILE] = jnp.where(survive, totals, 0.0)


def refreshed_slots(length, offs, parts, region_keep, residual, steps):
    slots = residual.shape[0]
    rows = slots // steps
    whole = lambda shape: pl.BlockSpec(shape, lambda i: (0, 0))
    return pl.pallas_call(
        refresh_kernel,
        out_shape=jax.ShapeDtypeStruct((slots, HEAD), jnp.float32),
        grid=(steps,),
        in_specs=[
            pl.BlockSpec(memory_space=pltpu.SMEM),
            whole(offs.shape),
            whole(parts.shape),
            whole(region_keep.shape),
            pl.BlockSpec((rows, HEAD), lambda i: (i, 0)),
        ],
        out_specs=pl.BlockSpec((rows, HEAD), lambda i: (i, 0)),
        compiler_params=pltpu.CompilerParams(vmem_limit_bytes=24 * MIB),
        cost_estimate=pl.CostEstimate(flops=3 * 10**9, bytes_accessed=4 * MIB, transcendentals=0),
        name="refreshed_slots",
    )(length, offs, parts, region_keep, residual)


def body(activations, kv_grads, kept_blocks, region_bounds, region_keep, residual):
    inputs = activations[0, 0]
    grad_cols = kv_grads[0, 0]
    keep_count = kept_blocks.shape[3]
    residual = residual[0, 0]
    regions = lax.axis_size("rep")
    pods = lax.axis_size("outer")
    column_blocks = grad_cols.shape[1] // HEAD
    spanned = residual.shape[0] // column_blocks + 1
    band = -(-(spanned + LANES - 1) // LANES) * LANES
    owner = lax.axis_index("rep")
    length = (region_bounds[owner + 1] - region_bounds[owner]).reshape(1)

    sent = send_rows(region_bounds, kept_blocks.reshape(1, keep_count), inputs, grad_cols, band)
    got = lax.all_to_all(
        sent.reshape(regions, CAP + 1, 1, HEAD), "rep", split_axis=0, concat_axis=0, tiled=True
    ).reshape(regions * (CAP + 1), HEAD)
    column, rows = kept_part(region_keep, residual)
    chosen, parts, offs = chosen_totals(got, column, rows)
    share = chosen.shape[0] // pods
    shares = lax.all_to_all(
        chosen.reshape(pods, share, HEAD), "outer", split_axis=0, concat_axis=0, tiled=True
    )
    merged = jnp.sum(shares, axis=0)
    refreshed = refreshed_slots(length, offs, parts, region_keep, residual, 3)
    return (merged[None], refreshed[None, None])


def solution(mesh):
    placed = (
        P("outer", "rep", None, None),
        P("outer", "rep", None, "tp"),
        P("outer", "rep", "tp", None),
        P(),
        P("rep", None),
        P("outer", "rep", None, "tp"),
    )
    return jax.shard_map(
        body,
        mesh=mesh,
        in_specs=placed,
        out_specs=(P("rep", "outer", "tp"), P("outer", "rep", None, "tp")),
        check_vma=False,
    )
```

time: 230 us -> 70.8 us (0.31)
  the two profiles are of different devices: /device:TPU:56 before, /device:TPU:64 now
where the time goes in v1:
time: 70.8 us; the launch traced here: 70.3 us
  waiting for transfers between devices  30.2 us (43%)
  starting transfers between devices  19.8 us (28%)
  Pallas kernels  11.1 us (16%)
  local copies, waits for them, and re-layouts  6.67 us (9%)
  between operations  1.91 us (3%)
    all_to_all x1, waiting for transfers between devices, body(): lax.all_to_all(sent.reshape(regions, CAP + 1, 1, HEAD), 'rep', split_axis...  26.1 us
    all_to_all x1, starting transfers between devices, body(): lax.all_to_all(sent.reshape(regions, CAP + 1, 1, HEAD), 'rep', split_axis...  12.7 us
    all_to_all x1, starting transfers between devices, body(): lax.all_to_all(chosen.reshape(pods, share, HEAD), 'outer', split_axis=0,...  7.1 us
    unnamed x18, local copies, waits for them, and re-layouts  6.08 us
    pallas_call x1, Pallas kernels, send_rows(): pl.pallas_call(functools.partial(send_kernel, band, 4), out_shape=jax.Sha...  5.23 us
    all_to_all x1, waiting for transfers between devices, body(): lax.all_to_all(chosen.reshape(pods, share, HEAD), 'outer', split_axis=0,...  4.14 us
    pallas_call x1, Pallas kernels, refreshed_slots(): pl.pallas_call(refresh_kernel, out_shape=jax.ShapeDtypeStruct((slots, HEA...  3.72 us
  transfers between devices with their start and end apart: 2, of which 2 were waited for; matrix products, arithmetic and copies ran while one was open for 1% of the time, Pallas kernels for 7%

profile of v1, /device:TPU:64, one launch (start us, length us, event | category | flops | bytes accessed | tf_op | source)
XLA Modules:
  0.0 70.3 jit_solution(2854986835427475789)
XLA Ops:
  0.6 0.0 copy-start.2
  0.6 0.6 copy-done.2
  1.3 0.0 copy-start.4
  1.3 1.6 %copy-done.4 = bf16[1,1,128,8192]{3,2,1,0:T(8,128)(2,1)S(1)} copy-done((bf16[1,1,128,8192]{3,2,1,0:T(8,128)(2,1)S(1)}, bf16[1,1,128,8192]{3,2,1,0:T(8,128)(2,1)}, u32[]{:S(2)}) %copy-start.4) | copy-done | bytes 2097176
  2.9 0.0 copy-start.7
  2.9 0.9 %copy-done.7 = bf16[1,1,128,1024]{3,2,1,0:T(8,128)(2,1)S(1)} copy-done((bf16[1,1,128,1024]{3,2,1,0:T(8,128)(2,1)S(1)}, bf16[1,1,128,1024]{3,2,1,0:T(8,128)(2,1)}, u32[]{:S(2)}) %copy-start.7) | copy-done | bytes 262168
  3.8 0.0 copy-start.8
  3.8 0.7 copy-done.8
  4.5 5.2 %send_rows.1 = f32[2080,128]{1,0:T(8,128)} custom-call(s32[33]{0:T(128)S(1)} %copy-done.2, s32[1,1024]{1,0:T(1,128)S(1)} %bitcast.14, bf16[128,8192]{1,0:T(8,128)(2,1)S(1)} %bitcast.12, bf16[128,1024]{1,0:T(8,128)(2,1)S(1)} %bitcast.13), custom_call_target="tpu_custom_call" | custom-call | flops 1000000000 | bytes 4194304 | tf_op jit(solution)/shard_map/send_rows/pallas_call | solution.py:98
  9.8 0.0 copy-start.3
  9.8 0.0 copy-start
  9.8 0.0 copy-start.1
  9.8 12.7 %all-to-all-start = ((f32[32,65,1,128]{3,2,1,0:T(1,128)}), f32[32,65,1,128]{3,2,1,0:T(1,128)S(1)}, u32[]{:S(2)}, u32[]{:S(2)}) async-start(f32[32,65,1,128]{3,2,1,0:T(1,128)} %bitcast.3), calls=%async_computation | async-start | bytes 2129920 | tf_op jit(solution)/shard_map/all_to_all | solution.py:241
  22.5 0.0 copy-done.3
  22.5 0.6 fusion
  24.3 0.0 copy-done
  24.3 0.0 copy-done.1
  24.3 1.0 %kept_part.1 = (f32[256,128]{1,0:T(8,128)S(1)}, f32[256,128]{1,0:T(8,128)S(1)}) custom-call(s32[1,256]{1,0:T(1,128)S(1)} %copy-done.1, s32[1,256]{1,0:T(1,128)S(1)} %copy-done.1, f32[2304,128]{1,0:T(8,128)S(1)} %bitcast.10), custom_call_target="tpu_custom_call" | custom-call | flops 100000000 | bytes 4194304 | tf_op jit(solution)/shard_map/kept_part/pallas_call | solution.py:129
  25.3 26.1 %all-to-all-done = f32[32,65,1,128]{3,2,1,0:T(1,128)S(1)} async-done(((f32[32,65,1,128]{3,2,1,0:T(1,128)}), f32[32,65,1,128]{3,2,1,0:T(1,128)S(1)}, u32[]{:S(2)}, u32[]{:S(2)}) %all-to-all-start) | async-done | bytes 1064992 | tf_op jit(solution)/shard_map/all_to_all | solution.py:241
  51.4 1.2 %chosen_totals.1 = (f32[256,128]{1,0:T(8,128)}, bf16[2048,256]{1,0:T(8,128)(2,1)S(1)}, f32[1,2048]{1,0:T(1,128)S(1)}) custom-call(f32[2080,128]{1,0:T(8,128)S(1)} %bitcast.9, f32[256,128]{1,0:T(8,128)S(1)} %get-tuple-element.7.column_ref, f32[256,128]{1,0:T(8,128)S(1)} %get-tuple-element.8.rows_ref), custom_call_target="tpu_custom_call" | custom-call | flops 100000000 | bytes 4194304 | tf_op jit(solution)/shard_map/chosen_totals/pallas_call | solution.py:164
  52.6 0.0 copy-start.5
  52.6 1.0 %copy-done.5 = bf16[2048,256]{1,0:T(8,128)(2,1)} copy-done((bf16[2048,256]{1,0:T(8,128)(2,1)}, bf16[2048,256]{1,0:T(8,128)(2,1)S(1)}, u32[]{:S(2)}) %copy-start.5) | copy-done | bytes 1048600
  53.5 7.1 %all-to-all-start.1 = ((f32[8,32,128]{2,1,0:T(8,128)}), f32[8,32,128]{2,1,0:T(8,128)S(1)}, u32[]{:S(2)}, u32[]{:S(2)}) async-start(f32[8,32,128]{2,1,0:T(8,128)} %bitcast.6), calls=%async_computation.1 | async-start | bytes 262144 | tf_op jit(solution)/shard_map/all_to_all | solution.py:247
  60.6 0.0 copy-start.6
  60.6 1.2 %copy-done.6 = bf16[2048,256]{1,0:T(8,128)(2,1)S(1)} copy-done((bf16[2048,256]{1,0:T(8,128)(2,1)S(1)}, bf16[2048,256]{1,0:T(8,128)(2,1)}, u32[]{:S(2)}) %copy-start.6) | copy-done | bytes 1048600
  61.9 3.7 %refreshed_slots.1 = f32[2304,128]{1,0:T(8,128)} custom-call(s32[1]{0:T(128)S(6)} %sub.4.length_ref, f32[1,2048]{1,0:T(1,128)S(1)} %get-tuple-element.10.offs_ref, bf16[2048,256]{1,0:T(8,128)(2,1)S(1)} %copy-done.6, s32[1,256]{1,0:T(1,128)S(1)} %copy-done.1, f32[2304,128]{1,0:T(8,128)S(1)} %bitcast.11), custom_call_target="tpu_custom_call" | custom-call | flops 3000000000 | bytes 4194304 | tf_op jit(solution)/shard_map/refreshed_slots/pallas_call | solution.py:209
  65.6 4.1 %all-to-all-done.1 = f32[8,32,128]{2,1,0:T(8,128)S(1)} async-done(((f32[8,32,128]{2,1,0:T(8,128)}), f32[8,32,128]{2,1,0:T(8,128)S(1)}, u32[]{:S(2)}, u32[]{:S(2)}) %all-to-all-start.1) | async-done | bytes 131104 | tf_op jit(solution)/shard_map/all_to_all | solution.py:247
  69.7 0.6 reduce_sum.9
Async XLA Ops:
  0.6 0.7 copy-start.2
  1.3 1.6 %copy-start.4 = (bf16[1,1,128,8192]{3,2,1,0:T(8,128)(2,1)S(1)}, bf16[1,1,128,8192]{3,2,1,0:T(8,128)(2,1)}, u32[]{:S(2)}) copy-start(bf16[1,1,128,8192]{3,2,1,0:T(8,128)(2,1)} %param.6) | copy-start | bytes 6291460
  2.9 0.9 %copy-start.7 = (bf16[1,1,128,1024]{3,2,1,0:T(8,128)(2,1)S(1)}, bf16[1,1,128,1024]{3,2,1,0:T(8,128)(2,1)}, u32[]{:S(2)}) copy-start(bf16[1,1,128,1024]{3,2,1,0:T(8,128)(2,1)} %param.7) | copy-start | bytes 786436
  3.8 0.7 copy-start.8
  9.8 12.7 %copy-start.3 = (s32[33]{0:T(128)S(1)}, s32[33]{0:T(128)}, u32[]{:S(2)}) copy-start(s32[33]{0:T(128)} %bounds_ref.1) | copy-start | bytes 400
  9.8 14.6 %copy-start = (f32[1,1,2304,128]{3,2,1,0:T(8,128)S(1)}, f32[1,1,2304,128]{3,2,1,0:T(8,128)}, u32[]{:S(2)}) copy-start(f32[1,1,2304,128]{3,2,1,0:T(8,128)} %param.11) | copy-start | bytes 3538948
  9.8 14.6 %copy-start.1 = (s32[1,256]{1,0:T(1,128)S(1)}, s32[1,256]{1,0:T(1,128)}, u32[]{:S(2)}) copy-start(s32[1,256]{1,0:T(1,128)} %keep_ref.3) | copy-start | bytes 3076
  9.8 41.6 %all-to-all-start = ((f32[32,65,1,128]{3,2,1,0:T(1,128)}), f32[32,65,1,128]{3,2,1,0:T(1,128)S(1)}, u32[]{:S(2)}, u32[]{:S(2)}) async-start(f32[32,65,1,128]{3,2,1,0:T(1,128)} %bitcast.3), calls=%async_computation | async-start | bytes 2129920 | tf_op jit(solution)/shard_map/all_to_all | solution.py:241
  52.6 1.0 %copy-start.5 = (bf16[2048,256]{1,0:T(8,128)(2,1)}, bf16[2048,256]{1,0:T(8,128)(2,1)S(1)}, u32[]{:S(2)}) copy-start(bf16[2048,256]{1,0:T(8,128)(2,1)S(1)} %get-tuple-element.11.parts_ref) | copy-start | bytes 3145732
  53.5 16.2 %all-to-all-start.1 = ((f32[8,32,128]{2,1,0:T(8,128)}), f32[8,32,128]{2,1,0:T(8,128)S(1)}, u32[]{:S(2)}, u32[]{:S(2)}) async-start(f32[8,32,128]{2,1,0:T(8,128)} %bitcast.6), calls=%async_computation.1 | async-start | bytes 262144 | tf_op jit(solution)/shard_map/all_to_all | solution.py:247
  60.6 1.2 %copy-start.6 = (bf16[2048,256]{1,0:T(8,128)(2,1)S(1)}, bf16[2048,256]{1,0:T(8,128)(2,1)}, u32[]{:S(2)}) copy-start(bf16[2048,256]{1,0:T(8,128)(2,1)} %copy-done.5) | copy-start | bytes 3145732

commit v2 on v1

--- a/solution.py
+++ b/solution.py
@@ -11,6 +11,7 @@
 CAP = 64
 LANES = 128
 SLOT_TILE = 256
+BATCH = 8
 MIB = 1 << 20
 CONTRACT_LAST = (((1,), (1,)), ((), ()))
 
@@ -19,7 +20,20 @@
     return lax.dot_general(left, right, CONTRACT_LAST, preferred_element_type=jnp.float32)
 
 
-def send_kernel(band, batch, bounds_ref, ids_ref, act_ref, grad_ref, out_ref):
+def send_kernel(
+    band, batch, bounds_hbm, ids_hbm, act_hbm, grad_hbm, out_hbm,
+    bounds_ref, ids_ref, act_ref, grad_ref, out_ref, sems, out_sems,
+):
+    loads = [
+        pltpu.make_async_copy(source, target, sems.at[place])
+        for place, (source, target) in enumerate(
+            ((bounds_hbm, bounds_ref), (ids_hbm, ids_ref), (act_hbm, act_ref), (grad_hbm, grad_ref))
+        )
+    ]
+    for load in loads:
+        load.start()
+    loads[0].wait()
+    loads[1].wait()
     regions = bounds_ref.shape[0] - 1
     keep_count = ids_ref.shape[1]
     width = act_ref.shape[1]
@@ -64,7 +78,10 @@
     offsets = jnp.where(by_region < 0.0, -1.0, by_region - starts.astype(jnp.float32))
 
     lane = lax.broadcasted_iota(jnp.int32, (CAP, LANES), 1)
+    loads[2].wait()
+    loads[3].wait()
     grads = grad_ref[...]
+    stores = []
     for first in range(0, regions, batch):
         columns, picked = [], []
         for region in range(first, first + batch):
@@ -90,17 +107,33 @@
             region = first + step
             out_ref[region * stride : region * stride + CAP, :] = block[step * CAP : (step + 1) * CAP]
             out_ref[region * stride + CAP : (region + 1) * stride, :] = offsets[region : region + 1]
+        done = pl.ds(first * stride, batch * stride)
+        store = pltpu.make_async_copy(out_ref.at[done], out_hbm.at[done], out_sems.at[first // batch])
+        store.start()
+        stores.append(store)
+    for store in stores:
+        store.wait()
 
 
 def send_rows(region_bounds, block_ids, inputs, grad_cols, band):
     regions = region_bounds.shape[0] - 1
-    vmem = pl.BlockSpec(memory_space=pltpu.VMEM)
+    hbm = pl.BlockSpec(memory_space=pltpu.HBM)
+    rows = regions * (CAP + 1)
     return pl.pallas_call(
-        functools.partial(send_kernel, band, 4),
-        out_shape=jax.ShapeDtypeStruct((regions * (CAP + 1), HEAD), jnp.float32),
-        in_specs=[pl.BlockSpec(memory_space=pltpu.SMEM), vmem, vmem, vmem],
-        out_specs=vmem,
-        compiler_params=pltpu.CompilerParams(vmem_limit_bytes=24 * MIB),
+        functools.partial(send_kernel, band, BATCH),
+        out_shape=jax.ShapeDtypeStruct((rows, HEAD), jnp.float32),
+        in_specs=[hbm] * 4,
+        out_specs=hbm,
+        scratch_shapes=[
+            pltpu.SMEM(region_bounds.shape, jnp.int32),
+            pltpu.VMEM(block_ids.shape, jnp.int32),
+            pltpu.VMEM(inputs.shape, inputs.dtype),
+            pltpu.VMEM(grad_cols.shape, grad_cols.dtype),
+            pltpu.VMEM((rows, HEAD), jnp.float32),
+            pltpu.SemaphoreType.DMA((4,)),
+            pltpu.SemaphoreType.DMA((regions // BATCH,)),
+        ],
+        compiler_params=pltpu.CompilerParams(vmem_limit_bytes=62 * MIB),
         cost_estimate=pl.CostEstimate(flops=10**9, bytes_accessed=4 * MIB, transcendentals=0),
         name="send_rows",
     )(region_bounds, block_ids, inputs, grad_cols)
@@ -137,72 +170,82 @@
     )(region_keep, region_keep, residual)
 
 
+def split_rows(got_ref, parts_ref, offs_ref):
+    stride = CAP + 1
+    lane = lax.broadcasted_iota(jnp.int32, (1, LANES), 1)
+    for pair in range(got_ref.shape[0] // stride // 2):
+        first = 2 * pair * stride
+        last = first + CAP
+        offs_ref[:, pair * LANES : (pair + 1) * LANES] = jnp.where(
+            lane < CAP, got_ref[last : last + 1], got_ref[last + stride : last + stride + 1]
+        )
+        for start, target in ((first, 2 * pair * CAP), (first + stride, (2 * pair + 1) * CAP)):
+            values = got_ref[start : start + CAP]
+            high = values.astype(jnp.bfloat16)
+            low = (values - high.astype(jnp.float32)).astype(jnp.bfloat16)
+            parts_ref[target : target + CAP, :HEAD] = high
+            parts_ref[target : target + CAP, HEAD:] = low
+
+
+def placed_sum(slots, offs_ref, parts_ref):
+    place = jnp.concatenate(
+        [
+            jnp.where(slots == offs_ref[:, part : part + LANES], 1.0, 0.0).astype(jnp.bfloat16)
+            for part in range(0, offs_ref.shape[1], LANES)
+        ],
+        axis=1,
+    )
+    summed = jnp.dot(place, parts_ref[...], preferred_element_type=jnp.float32)
+    return summed[:, :HEAD] + summed[:, HEAD:]
+
+
 def chosen_kernel(got_ref, column_ref, rows_ref, chosen_ref, parts_ref, offs_ref):
-    sources = got_ref.shape[0] // (CAP + 1)
-    stride = CAP + 1
-    column = column_ref[...]
-    lane = lax.broadcasted_iota(jnp.int32, (1, LANES), 1)
-    places = []
-    for pair in range(sources // 2):
-        first = 2 * pair * stride + CAP
-        offs = jnp.where(lane < CAP, got_ref[first : first + 1], got_ref[first + stride : first + stride + 1])
-        offs_ref[:, pair * LANES : (pair + 1) * LANES] = offs
-        places.append(jnp.where(column == offs, 1.0, 0.0).astype(jnp.bfloat16))
-    for source in range(sources):
-        values = got_ref[source * stride : source * stride + CAP]
-        high = values.astype(jnp.bfloat16)
-        low = (values - high.astype(jnp.float32)).astype(jnp.bfloat16)
-        parts_ref[source * CAP : (source + 1) * CAP, :HEAD] = high
-        parts_ref[source * CAP : (source + 1) * CAP, HEAD:] = low
-    summed = jnp.dot(jnp.concatenate(places, axis=1), parts_ref[...], preferred_element_type=jnp.float32)
-    chosen_ref[...] = summed[:, :HEAD] + summed[:, HEAD:] + rows_ref[...]
+    split_rows(got_ref, parts_ref, offs_ref)
+    chosen_ref[...] = placed_sum(column_ref[...], offs_ref, parts_ref) + rows_ref[...]
+
+
+def part_scratch(got):
+    filled = got.shape[0] // (CAP + 1) * CAP
+    return [pltpu.VMEM((filled, 2 * HEAD), jnp.bfloat16), pltpu.VMEM((1, filled), jnp.float32)]
 
 
 def chosen_totals(got, column, rows):
-    sources = got.shape[0] // (CAP + 1)
     vmem = pl.BlockSpec(memory_space=pltpu.VMEM)
     return pl.pallas_call(
         chosen_kernel,
-        out_shape=[
-            jax.ShapeDtypeStruct(rows.shape, jnp.float32),
-            jax.ShapeDtypeStruct((sources * CAP, 2 * HEAD), jnp.bfloat16),
-            jax.ShapeDtypeStruct((1, sources * CAP), jnp.float32),
-        ],
+        out_shape=jax.ShapeDtypeStruct(rows.shape, jnp.float32),
         in_specs=[vmem] * 3,
-        out_specs=[vmem] * 3,
+        out_specs=vmem,
+        scratch_shapes=part_scratch(got),
         compiler_params=pltpu.CompilerParams(vmem_limit_bytes=16 * MIB),
         cost_estimate=pl.CostEstimate(flops=10**8, bytes_accessed=4 * MIB, transcendentals=0),
         name="chosen_totals",
     )(got, column, rows)
 
 
-def refresh_kernel(length_ref, offs_ref, parts_ref, keep_ref, residual_ref, out_ref):
+def refresh_kernel(length_ref, got_ref, keep_ref, residual_ref, out_ref, parts_ref, offs_ref):
     rows = out_ref.shape[0]
     base = pl.program_id(0) * rows
     length = length_ref[0]
-    parts = parts_ref[...]
     keep = keep_ref[...]
+
+    @pl.when(base == 0)
+    def _():
+        split_rows(got_ref, parts_ref, offs_ref)
+
     for first in range(0, rows, SLOT_TILE):
         slot = lax.broadcasted_iota(jnp.int32, (SLOT_TILE, LANES), 0) + (base + first)
-        slot_f = slot.astype(jnp.float32)
-        place = jnp.concatenate(
-            [
-                jnp.where(slot_f == offs_ref[:, part : part + LANES], 1.0, 0.0).astype(jnp.bfloat16)
-                for part in range(0, offs_ref.shape[1], LANES)
-            ],
-            axis=1,
-        )
-        summed = jnp.dot(place, parts, preferred_element_type=jnp.float32)
         hits = jnp.zeros((SLOT_TILE, LANES), jnp.float32)
         for part in range(0, keep.shape[1], LANES):
             hits = hits + jnp.where(slot == keep[:, part : part + LANES], 1.0, 0.0)
         named = jnp.sum(hits, axis=1, keepdims=True)
         survive = (slot < length) & (jnp.broadcast_to(named, slot.shape) == 0.0)
-        totals = summed[:, :HEAD] + summed[:, HEAD:] + residual_ref[first : first + SLOT_TILE]
+        summed = placed_sum(slot.astype(jnp.float32), offs_ref, parts_ref)
+        totals = summed + residual_ref[first : first + SLOT_TILE]
         out_ref[first : first + SLOT_TILE] = jnp.where(survive, totals, 0.0)
 
 
-def refreshed_slots(length, offs, parts, region_keep, residual, steps):
+def refreshed_slots(length, got, region_keep, residual, steps):
     slots = residual.shape[0]
     rows = slots // steps
     whole = lambda shape: pl.BlockSpec(shape, lambda i: (0, 0))
@@ -212,16 +255,16 @@
         grid=(steps,),
         in_specs=[
             pl.BlockSpec(memory_space=pltpu.SMEM),
-            whole(offs.shape),
-            whole(parts.shape),
+            pl.BlockSpec(memory_space=pltpu.VMEM),
             whole(region_keep.shape),
             pl.BlockSpec((rows, HEAD), lambda i: (i, 0)),
         ],
         out_specs=pl.BlockSpec((rows, HEAD), lambda i: (i, 0)),
+        scratch_shapes=part_scratch(got),
         compiler_params=pltpu.CompilerParams(vmem_limit_bytes=24 * MIB),
         cost_estimate=pl.CostEstimate(flops=3 * 10**9, bytes_accessed=4 * MIB, transcendentals=0),
         name="refreshed_slots",
-    )(length, offs, parts, region_keep, residual)
+    )(length, got, region_keep, residual)
 
 
 def body(activations, kv_grads, kept_blocks, region_bounds, region_keep, residual):
@@ -242,13 +285,13 @@
         sent.reshape(regions, CAP + 1, 1, HEAD), "rep", split_axis=0, concat_axis=0, tiled=True
     ).reshape(regions * (CAP + 1), HEAD)
     column, rows = kept_part(region_keep, residual)
-    chosen, parts, offs = chosen_totals(got, column, rows)
+    chosen = chosen_totals(got, column, rows)
     share = chosen.shape[0] // pods
     shares = lax.all_to_all(
         chosen.reshape(pods, share, HEAD), "outer", split_axis=0, concat_axis=0, tiled=True
     )
     merged = jnp.sum(shares, axis=0)
-    refreshed = refreshed_slots(length, offs, parts, region_keep, residual, 3)
+    refreshed = refreshed_slots(length, got, region_keep, residual, 3)
     return (merged[None], refreshed[None, None])
 
 

time: 70.8 us -> 65.7 us (0.928)
  local copies, waits for them, and re-layouts: 6.67 us -> 0.69 us
  waiting for transfers between devices: 30.2 us -> 31 us
    unnamed x18 -> x6, local copies, waits for them, and re-layouts: 6.08 us -> 0.02 us
    all_to_all x1, waiting for transfers between devices: 4.14 us -> 5.12 us  [body(): lax.all_to_all(chosen.reshape(pods, share, HEAD), 'outer', split_axis=0,...]
  transfers between devices with their start and end apart: 2 -> 2, of which waited for: 2 -> 2; matrix products, arithmetic and copies ran while one was open for 1% -> 1% of each run, Pallas kernels for 7% -> 8%
where the time goes in v2:
time: 65.7 us; the launch traced here: 65.4 us
  waiting for transfers between devices  31 us (47%)
  starting transfers between devices  19.8 us (30%)
  Pallas kernels  11.2 us (17%)
  between operations  2.05 us (3%)
  local copies, waits for them, and re-layouts  0.69 us (1%)
    all_to_all x1, waiting for transfers between devices, body(): lax.all_to_all(sent.reshape(regions, CAP + 1, 1, HEAD), 'rep', split_axis...  25.8 us
    all_to_all x1, starting transfers between devices, body(): lax.all_to_all(sent.reshape(regions, CAP + 1, 1, HEAD), 'rep', split_axis...  12.7 us
    all_to_all x1, starting transfers between devices, body(): lax.all_to_all(chosen.reshape(pods, share, HEAD), 'outer', split_axis=0,...  7.09 us
    pallas_call x1, Pallas kernels, send_rows(): pl.pallas_call(functools.partial(send_kernel, band, BATCH), out_shape=jax...  5.12 us
    all_to_all x1, waiting for transfers between devices, body(): lax.all_to_all(chosen.reshape(pods, share, HEAD), 'outer', split_axis=0,...  5.12 us
    pallas_call x1, Pallas kernels, refreshed_slots(): pl.pallas_call(refresh_kernel, out_shape=jax.ShapeDtypeStruct((slots, HEA...  3.96 us
  transfers between devices with their start and end apart: 2, of which 2 were waited for; matrix products, arithmetic and copies ran while one was open for 1% of the time, Pallas kernels for 8%

profile of v2, /device:TPU:64, one launch (start us, length us, event | category | flops | bytes accessed | tf_op | source)
XLA Modules:
  0.0 65.4 jit_solution(3817368987539225391)
XLA Ops:
  0.6 5.1 %send_rows.1 = f32[2080,128]{1,0:T(8,128)} custom-call(s32[33]{0:T(128)} %bounds_hbm.1, s32[1,1024]{1,0:T(1,128)} %bitcast.17, bf16[128,8192]{1,0:T(8,128)(2,1)} %bitcast.15, bf16[128,1024]{1,0:T(8,128)(2,1)} %bitcast.16), custom_call_target="tpu_custom_call" | custom-call | flops 1000000000 | bytes 4194304 | tf_op jit(solution)/shard_map/send_rows/pallas_call | solution.py:122
  5.8 0.0 copy-start.2
  5.8 0.0 copy-start
  5.8 0.0 copy-start.1
  5.8 12.7 %all-to-all-start = ((f32[32,65,1,128]{3,2,1,0:T(1,128)}), f32[32,65,1,128]{3,2,1,0:T(1,128)S(1)}, u32[]{:S(2)}, u32[]{:S(2)}) async-start(f32[32,65,1,128]{3,2,1,0:T(1,128)} %bitcast.13), calls=%async_computation | async-start | bytes 2129920 | tf_op jit(solution)/shard_map/all_to_all | solution.py:284
  18.5 0.0 copy-done.2
  18.6 0.7 %fusion = (s32[1]{0:T(128)}, s32[1]{0:T(128)}) fusion(s32[33]{0:T(128)S(1)} %copy-done.2, s32[]{:T(128)S(6)} %select_n.7, s32[]{:T(128)S(6)} %select_n.6), kind=kLoop, calls=%fused_computation | loop fusion | bytes 24 | tf_op jit(solution)/shard_map/dynamic_slice | solution.py:281
  20.6 0.0 copy-done
  20.6 0.0 copy-done.1
  20.6 1.0 %kept_part.1 = (f32[256,128]{1,0:T(8,128)S(1)}, f32[256,128]{1,0:T(8,128)S(1)}) custom-call(s32[1,256]{1,0:T(1,128)S(1)} %copy-done.1, s32[1,256]{1,0:T(1,128)S(1)} %copy-done.1, f32[2304,128]{1,0:T(8,128)S(1)} %bitcast.11), custom_call_target="tpu_custom_call" | custom-call | flops 100000000 | bytes 4194304 | tf_op jit(solution)/shard_map/kept_part/pallas_call | solution.py:162
  21.6 25.8 %all-to-all-done = f32[32,65,1,128]{3,2,1,0:T(1,128)S(1)} async-done(((f32[32,65,1,128]{3,2,1,0:T(1,128)}), f32[32,65,1,128]{3,2,1,0:T(1,128)S(1)}, u32[]{:S(2)}, u32[]{:S(2)}) %all-to-all-start) | async-done | bytes 1064992 | tf_op jit(solution)/shard_map/all_to_all | solution.py:284
  47.4 1.2 %chosen_totals.1 = f32[256,128]{1,0:T(8,128)} custom-call(f32[2080,128]{1,0:T(8,128)S(1)} %bitcast.9, f32[256,128]{1,0:T(8,128)S(1)} %get-tuple-element.4.column_ref, f32[256,128]{1,0:T(8,128)S(1)} %get-tuple-element.5.rows_ref), custom_call_target="tpu_custom_call" | custom-call | flops 100000000 | bytes 4194304 | tf_op jit(solution)/shard_map/chosen_totals/pallas_call | solution.py:214
  48.6 7.1 %all-to-all-start.1 = ((f32[8,32,128]{2,1,0:T(8,128)}), f32[8,32,128]{2,1,0:T(8,128)S(1)}, u32[]{:S(2)}, u32[]{:S(2)}) async-start(f32[8,32,128]{2,1,0:T(8,128)} %bitcast.6), calls=%async_computation.1 | async-start | bytes 262144 | tf_op jit(solution)/shard_map/all_to_all | solution.py:290
  55.7 4.0 %refreshed_slots.1 = f32[2304,128]{1,0:T(8,128)} custom-call(s32[1]{0:T(128)S(6)} %sub.4.length_ref, f32[2080,128]{1,0:T(8,128)S(1)} %bitcast.10, s32[1,256]{1,0:T(1,128)S(1)} %copy-done.1, f32[2304,128]{1,0:T(8,128)S(1)} %bitcast.12), custom_call_target="tpu_custom_call" | custom-call | flops 3000000000 | bytes 4194304 | tf_op jit(solution)/shard_map/refreshed_slots/pallas_call | solution.py:252
  59.7 5.1 %all-to-all-done.1 = f32[8,32,128]{2,1,0:T(8,128)S(1)} async-done(((f32[8,32,128]{2,1,0:T(8,128)}), f32[8,32,128]{2,1,0:T(8,128)S(1)}, u32[]{:S(2)}, u32[]{:S(2)}) %all-to-all-start.1) | async-done | bytes 131104 | tf_op jit(solution)/shard_map/all_to_all | solution.py:290
  64.8 0.6 reduce_sum.9
Async XLA Ops:
  5.8 12.8 %copy-start.2 = (s32[33]{0:T(128)S(1)}, s32[33]{0:T(128)}, u32[]{:S(2)}) copy-start(s32[33]{0:T(128)} %bounds_hbm.1) | copy-start | bytes 400
  5.8 14.8 %copy-start = (f32[1,1,2304,128]{3,2,1,0:T(8,128)S(1)}, f32[1,1,2304,128]{3,2,1,0:T(8,128)}, u32[]{:S(2)}) copy-start(f32[1,1,2304,128]{3,2,1,0:T(8,128)} %param.11) | copy-start | bytes 3538948
  5.8 14.8 %copy-start.1 = (s32[1,256]{1,0:T(1,128)S(1)}, s32[1,256]{1,0:T(1,128)}, u32[]{:S(2)}) copy-start(s32[1,256]{1,0:T(1,128)} %keep_ref.3) | copy-start | bytes 3076
  5.8 41.6 %all-to-all-start = ((f32[32,65,1,128]{3,2,1,0:T(1,128)}), f32[32,65,1,128]{3,2,1,0:T(1,128)S(1)}, u32[]{:S(2)}, u32[]{:S(2)}) async-start(f32[32,65,1,128]{3,2,1,0:T(1,128)} %bitcast.13), calls=%async_computation | async-start | bytes 2129920 | tf_op jit(solution)/shard_map/all_to_all | solution.py:284
  48.6 16.2 %all-to-all-start.1 = ((f32[8,32,128]{2,1,0:T(8,128)}), f32[8,32,128]{2,1,0:T(8,128)S(1)}, u32[]{:S(2)}, u32[]{:S(2)}) async-start(f32[8,32,128]{2,1,0:T(8,128)} %bitcast.6), calls=%async_computation.1 | async-start | bytes 262144 | tf_op jit(solution)/shard_map/all_to_all | solution.py:290

commit v3 on v2

--- a/solution.py
+++ b/solution.py
@@ -21,13 +21,20 @@
 
 
 def send_kernel(
-    band, batch, bounds_hbm, ids_hbm, act_hbm, grad_hbm, out_hbm,
+    region_rows, band, batch, bounds_hbm, ids_hbm, act_hbm, grad_hbm, out_hbm,
     bounds_ref, ids_ref, act_ref, grad_ref, out_ref, sems, out_sems,
 ):
+    half = act_ref.shape[1] // 2
     loads = [
         pltpu.make_async_copy(source, target, sems.at[place])
         for place, (source, target) in enumerate(
-            ((bounds_hbm, bounds_ref), (ids_hbm, ids_ref), (act_hbm, act_ref), (grad_hbm, grad_ref))
+            (
+                (bounds_hbm, bounds_ref),
+                (ids_hbm, ids_ref),
+                (act_hbm.at[:, pl.ds(0, half)], act_ref.at[:, pl.ds(0, half)]),
+                (grad_hbm, grad_ref),
+                (act_hbm.at[:, pl.ds(half, half)], act_ref.at[:, pl.ds(half, half)]),
+            )
         )
     ]
     for load in loads:
@@ -77,32 +84,54 @@
     by_rank = 256.0 * contract_last(ranked, high_part) + contract_last(ranked, low_part) - 1.0
     offsets = jnp.where(by_region < 0.0, -1.0, by_region - starts.astype(jnp.float32))
 
-    lane = lax.broadcasted_iota(jnp.int32, (CAP, LANES), 1)
-    loads[2].wait()
+    lane = lax.broadcasted_iota(jnp.int32, (2 * CAP, LANES), 1)
     loads[3].wait()
-    grads = grad_ref[...]
+    act_loads, waited = (loads[2], loads[4]), 0
+    lane_low = lane.astype(jnp.bfloat16)
+    paired = jnp.concatenate(
+        [
+            jnp.concatenate(
+                [grad_ref[:, column * HEAD : (column + 1) * HEAD] for column in range(parity, column_blocks, 2)],
+                axis=1,
+            )
+            for parity in range(2)
+        ],
+        axis=0,
+    )
     stores = []
     for first in range(0, regions, batch):
         columns, picked = [], []
-        for region in range(first, first + batch):
-            wanted = jnp.broadcast_to(by_rank[:, region : region + 1], (CAP, LANES)).astype(jnp.int32)
+        reach = min(width, (first + batch) * region_rows + band)
+        while waited < len(act_loads) and reach > waited * half:
+            act_loads[waited].wait()
+            waited += 1
+        for region in range(first, first + batch, 2):
+            wanted = jnp.concatenate(
+                [jnp.broadcast_to(by_rank[:, r : r + 1], (CAP, LANES)) for r in (region, region + 1)], axis=0
+            ).astype(jnp.int32)
             base = (bounds_ref[region] >> column_bits) & ~(LANES - 1)
             base = pl.multiple_of(jnp.minimum(base, width - band), LANES)
             place = (wanted >> column_bits) - base
             columns.append(wanted & (column_blocks - 1))
+            low = (place & (LANES - 1)).astype(jnp.bfloat16)
+            high = (place >> 7).astype(jnp.bfloat16)
+            zero = jnp.zeros(low.shape, jnp.bfloat16)
+            one = jnp.ones(low.shape, jnp.bfloat16)
+            hot = jnp.where(low == lane_low, high, zero - 1)
             chosen = jnp.concatenate(
-                [
-                    jnp.where(lane + part == place, 1.0, 0.0).astype(jnp.bfloat16)
-                    for part in range(0, band, LANES)
-                ],
-                axis=1,
+                [jnp.where(hot == part, one, zero) for part in range(band // LANES)], axis=1
             )
             picked.append(contract_last(chosen, act_ref[:, pl.ds(base, band)]).astype(jnp.bfloat16))
         columns = jnp.concatenate(columns, axis=0)
-        wide = jnp.dot(jnp.concatenate(picked, axis=0), grads, preferred_element_type=jnp.float32)
+        rows = jnp.concatenate(picked, axis=0)
+        odd = (columns & 1).astype(jnp.bfloat16)
+        zero = jnp.zeros_like(rows)
+        spread = jnp.concatenate([jnp.where(odd == 0, rows, zero), jnp.where(odd == 0, zero, rows)], axis=1)
+        wide = jnp.dot(spread, paired, preferred_element_type=jnp.float32)
+        pair = columns >> 1
         block = wide[:, :HEAD]
-        for column in range(1, column_blocks):
-            block = jnp.where(columns == column, wide[:, column * HEAD : (column + 1) * HEAD], block)
+        for place in range(1, column_blocks // 2):
+            block = jnp.where(pair == place, wide[:, place * HEAD : (place + 1) * HEAD], block)
         for step in range(batch):
             region = first + step
             out_ref[region * stride : region * stride + CAP, :] = block[step * CAP : (step + 1) * CAP]
@@ -115,12 +144,13 @@
         store.wait()
 
 
-def send_rows(region_bounds, block_ids, inputs, grad_cols, band):
+def send_rows(region_bounds, block_ids, inputs, grad_cols, region_rows):
     regions = region_bounds.shape[0] - 1
     hbm = pl.BlockSpec(memory_space=pltpu.HBM)
     rows = regions * (CAP + 1)
+    band = -(-(2 * region_rows + LANES) // (2 * LANES)) * (2 * LANES)
     return pl.pallas_call(
-        functools.partial(send_kernel, band, BATCH),
+        functools.partial(send_kernel, region_rows, band, BATCH),
         out_shape=jax.ShapeDtypeStruct((rows, HEAD), jnp.float32),
         in_specs=[hbm] * 4,
         out_specs=hbm,
@@ -130,7 +160,7 @@
             pltpu.VMEM(inputs.shape, inputs.dtype),
             pltpu.VMEM(grad_cols.shape, grad_cols.dtype),
             pltpu.VMEM((rows, HEAD), jnp.float32),
-            pltpu.SemaphoreType.DMA((4,)),
+            pltpu.SemaphoreType.DMA((5,)),
             pltpu.SemaphoreType.DMA((regions // BATCH,)),
         ],
         compiler_params=pltpu.CompilerParams(vmem_limit_bytes=62 * MIB),
@@ -275,12 +305,11 @@
     regions = lax.axis_size("rep")
     pods = lax.axis_size("outer")
     column_blocks = grad_cols.shape[1] // HEAD
-    spanned = residual.shape[0] // column_blocks + 1
-    band = -(-(spanned + LANES - 1) // LANES) * LANES
+    region_rows = residual.shape[0] // column_blocks
     owner = lax.axis_index("rep")
     length = (region_bounds[owner + 1] - region_bounds[owner]).reshape(1)
 
-    sent = send_rows(region_bounds, kept_blocks.reshape(1, keep_count), inputs, grad_cols, band)
+    sent = send_rows(region_bounds, kept_blocks.reshape(1, keep_count), inputs, grad_cols, region_rows)
     got = lax.all_to_all(
         sent.reshape(regions, CAP + 1, 1, HEAD), "rep", split_axis=0, concat_axis=0, tiled=True
     ).reshape(regions * (CAP + 1), HEAD)

time: 65.7 us -> 64.7 us (0.985)
  Pallas kernels: 11.2 us -> 10.2 us
    pallas_call x1, Pallas kernels: 5.12 us -> 4.11 us  [send_rows(): pl.pallas_call(functools.partial(send_kernel, region_rows, band, BATCH),...]
where the time goes in v3:
time: 64.7 us; the launch traced here: 64.4 us
  waiting for transfers between devices  31 us (48%)
  starting transfers between devices  19.8 us (31%)
  Pallas kernels  10.2 us (16%)
  between operations  2.05 us (3%)
  local copies, waits for them, and re-layouts  0.69 us (1%)
    all_to_all x1, waiting for transfers between devices, body(): lax.all_to_all(sent.reshape(regions, CAP + 1, 1, HEAD), 'rep', split_axis...  25.8 us
    all_to_all x1, starting transfers between devices, body(): lax.all_to_all(sent.reshape(regions, CAP + 1, 1, HEAD), 'rep', split_axis...  12.7 us
    all_to_all x1, starting transfers between devices, body(): lax.all_to_all(chosen.reshape(pods, share, HEAD), 'outer', split_axis=0,...  7.1 us
    all_to_all x1, waiting for transfers between devices, body(): lax.all_to_all(chosen.reshape(pods, share, HEAD), 'outer', split_axis=0,...  5.12 us
    pallas_call x1, Pallas kernels, send_rows(): pl.pallas_call(functools.partial(send_kernel, region_rows, band, BATCH),...  4.11 us
    pallas_call x1, Pallas kernels, refreshed_slots(): pl.pallas_call(refresh_kernel, out_shape=jax.ShapeDtypeStruct((slots, HEA...  3.96 us
  transfers between devices with their start and end apart: 2, of which 2 were waited for; matrix products, arithmetic and copies ran while one was open for 1% of the time, Pallas kernels for 8%

profile of v3, /device:TPU:64, one launch (start us, length us, event | category | flops | bytes accessed | tf_op | source)
XLA Modules:
  0.0 64.4 jit_solution(10113854424365111835)
XLA Ops:
  0.6 4.1 %send_rows.1 = f32[2080,128]{1,0:T(8,128)} custom-call(s32[33]{0:T(128)} %bounds_hbm.1, s32[1,1024]{1,0:T(1,128)} %bitcast.17, bf16[128,8192]{1,0:T(8,128)(2,1)} %bitcast.15, bf16[128,1024]{1,0:T(8,128)(2,1)} %bitcast.16), custom_call_target="tpu_custom_call" | custom-call | flops 1000000000 | bytes 4194304 | tf_op jit(solution)/shard_map/send_rows/pallas_call | solution.py:152
  4.7 0.0 copy-start.2
  4.8 0.0 copy-start
  4.8 0.0 copy-start.1
  4.8 12.7 %all-to-all-start = ((f32[32,65,1,128]{3,2,1,0:T(1,128)}), f32[32,65,1,128]{3,2,1,0:T(1,128)S(1)}, u32[]{:S(2)}, u32[]{:S(2)}) async-start(f32[32,65,1,128]{3,2,1,0:T(1,128)} %bitcast.13), calls=%async_computation | async-start | bytes 2129920 | tf_op jit(solution)/shard_map/all_to_all | solution.py:313
  17.5 0.0 copy-done.2
  17.5 0.7 %fusion = (s32[1]{0:T(128)}, s32[1]{0:T(128)}) fusion(s32[33]{0:T(128)S(1)} %copy-done.2, s32[]{:T(128)S(6)} %select_n.7, s32[]{:T(128)S(6)} %select_n.6), kind=kLoop, calls=%fused_computation | loop fusion | bytes 24 | tf_op jit(solution)/shard_map/dynamic_slice | solution.py:310
  19.5 0.0 copy-done
  19.6 0.0 copy-done.1
  19.6 1.0 %kept_part.1 = (f32[256,128]{1,0:T(8,128)S(1)}, f32[256,128]{1,0:T(8,128)S(1)}) custom-call(s32[1,256]{1,0:T(1,128)S(1)} %copy-done.1, s32[1,256]{1,0:T(1,128)S(1)} %copy-done.1, f32[2304,128]{1,0:T(8,128)S(1)} %bitcast.11), custom_call_target="tpu_custom_call" | custom-call | flops 100000000 | bytes 4194304 | tf_op jit(solution)/shard_map/kept_part/pallas_call | solution.py:192
  20.5 25.8 %all-to-all-done = f32[32,65,1,128]{3,2,1,0:T(1,128)S(1)} async-done(((f32[32,65,1,128]{3,2,1,0:T(1,128)}), f32[32,65,1,128]{3,2,1,0:T(1,128)S(1)}, u32[]{:S(2)}, u32[]{:S(2)}) %all-to-all-start) | async-done | bytes 1064992 | tf_op jit(solution)/shard_map/all_to_all | solution.py:313
  46.4 1.2 %chosen_totals.1 = f32[256,128]{1,0:T(8,128)} custom-call(f32[2080,128]{1,0:T(8,128)S(1)} %bitcast.9, f32[256,128]{1,0:T(8,128)S(1)} %get-tuple-element.4.column_ref, f32[256,128]{1,0:T(8,128)S(1)} %get-tuple-element.5.rows_ref), custom_call_target="tpu_custom_call" | custom-call | flops 100000000 | bytes 4194304 | tf_op jit(solution)/shard_map/chosen_totals/pallas_call | solution.py:244
  47.6 7.1 %all-to-all-start.1 = ((f32[8,32,128]{2,1,0:T(8,128)}), f32[8,32,128]{2,1,0:T(8,128)S(1)}, u32[]{:S(2)}, u32[]{:S(2)}) async-start(f32[8,32,128]{2,1,0:T(8,128)} %bitcast.6), calls=%async_computation.1 | async-start | bytes 262144 | tf_op jit(solution)/shard_map/all_to_all | solution.py:319
  54.7 4.0 %refreshed_slots.1 = f32[2304,128]{1,0:T(8,128)} custom-call(s32[1]{0:T(128)S(6)} %sub.4.length_ref, f32[2080,128]{1,0:T(8,128)S(1)} %bitcast.10, s32[1,256]{1,0:T(1,128)S(1)} %copy-done.1, f32[2304,128]{1,0:T(8,128)S(1)} %bitcast.12), custom_call_target="tpu_custom_call" | custom-call | flops 3000000000 | bytes 4194304 | tf_op jit(solution)/shard_map/refreshed_slots/pallas_call | solution.py:282
  58.6 5.1 %all-to-all-done.1 = f32[8,32,128]{2,1,0:T(8,128)S(1)} async-done(((f32[8,32,128]{2,1,0:T(8,128)}), f32[8,32,128]{2,1,0:T(8,128)S(1)}, u32[]{:S(2)}, u32[]{:S(2)}) %all-to-all-start.1) | async-done | bytes 131104 | tf_op jit(solution)/shard_map/all_to_all | solution.py:319
  63.8 0.6 reduce_sum.9
Async XLA Ops:
  4.7 12.8 %copy-start.2 = (s32[33]{0:T(128)S(1)}, s32[33]{0:T(128)}, u32[]{:S(2)}) copy-start(s32[33]{0:T(128)} %bounds_hbm.1) | copy-start | bytes 400
  4.8 14.8 %copy-start = (f32[1,1,2304,128]{3,2,1,0:T(8,128)S(1)}, f32[1,1,2304,128]{3,2,1,0:T(8,128)}, u32[]{:S(2)}) copy-start(f32[1,1,2304,128]{3,2,1,0:T(8,128)} %param.11) | copy-start | bytes 3538948
  4.8 14.8 %copy-start.1 = (s32[1,256]{1,0:T(1,128)S(1)}, s32[1,256]{1,0:T(1,128)}, u32[]{:S(2)}) copy-start(s32[1,256]{1,0:T(1,128)} %keep_ref.3) | copy-start | bytes 3076
  4.8 41.6 %all-to-all-start = ((f32[32,65,1,128]{3,2,1,0:T(1,128)}), f32[32,65,1,128]{3,2,1,0:T(1,128)S(1)}, u32[]{:S(2)}, u32[]{:S(2)}) async-start(f32[32,65,1,128]{3,2,1,0:T(1,128)} %bitcast.13), calls=%async_computation | async-start | bytes 2129920 | tf_op jit(solution)/shard_map/all_to_all | solution.py:313
  47.6 16.2 %all-to-all-start.1 = ((f32[8,32,128]{2,1,0:T(8,128)}), f32[8,32,128]{2,1,0:T(8,128)S(1)}, u32[]{:S(2)}, u32[]{:S(2)}) async-start(f32[8,32,128]{2,1,0:T(8,128)} %bitcast.6), calls=%async_computation.1 | async-start | bytes 262144 | tf_op jit(solution)/shard_map/all_to_all | solution.py:319

commit v4 on v3

--- a/solution.py
+++ b/solution.py
@@ -18,6 +18,10 @@
 
 def contract_last(left, right):
     return lax.dot_general(left, right, CONTRACT_LAST, preferred_element_type=jnp.float32)
+
+
+def seating(regions):
+    return [regions - 1 - seat for seat in range(regions)]
 
 
 def send_kernel(
@@ -46,6 +50,7 @@
     width = act_ref.shape[1]
     column_blocks = grad_ref.shape[1] // HEAD
     column_bits = column_blocks.bit_length() - 1
+    seats = seating(regions)
     chunks = keep_count // LANES
     stride = CAP + 1
 
@@ -98,7 +103,7 @@
         ],
         axis=0,
     )
-    stores = []
+    held = []
     for first in range(0, regions, batch):
         columns, picked = [], []
         reach = min(width, (first + batch) * region_rows + band)
@@ -122,8 +127,10 @@
                 [jnp.where(hot == part, one, zero) for part in range(band // LANES)], axis=1
             )
             picked.append(contract_last(chosen, act_ref[:, pl.ds(base, band)]).astype(jnp.bfloat16))
-        columns = jnp.concatenate(columns, axis=0)
-        rows = jnp.concatenate(picked, axis=0)
+        held.append((first, jnp.concatenate(columns, axis=0), jnp.concatenate(picked, axis=0)))
+
+    stores = []
+    for first, columns, rows in held:
         odd = (columns & 1).astype(jnp.bfloat16)
         zero = jnp.zeros_like(rows)
         spread = jnp.concatenate([jnp.where(odd == 0, rows, zero), jnp.where(odd == 0, zero, rows)], axis=1)
@@ -134,9 +141,11 @@
             block = jnp.where(pair == place, wide[:, place * HEAD : (place + 1) * HEAD], block)
         for step in range(batch):
             region = first + step
-            out_ref[region * stride : region * stride + CAP, :] = block[step * CAP : (step + 1) * CAP]
-            out_ref[region * stride + CAP : (region + 1) * stride, :] = offsets[region : region + 1]
-        done = pl.ds(first * stride, batch * stride)
+            seat = seats.index(region)
+            out_ref[seat * stride : seat * stride + CAP, :] = block[step * CAP : (step + 1) * CAP]
+            out_ref[seat * stride + CAP : (seat + 1) * stride, :] = offsets[region : region + 1]
+        block_first = min(seats.index(region) for region in range(first, first + batch))
+        done = pl.ds(block_first * stride, batch * stride)
         store = pltpu.make_async_copy(out_ref.at[done], out_hbm.at[done], out_sems.at[first // batch])
         store.start()
         stores.append(store)
@@ -311,7 +320,12 @@
 
     sent = send_rows(region_bounds, kept_blocks.reshape(1, keep_count), inputs, grad_cols, region_rows)
     got = lax.all_to_all(
-        sent.reshape(regions, CAP + 1, 1, HEAD), "rep", split_axis=0, concat_axis=0, tiled=True
+        sent.reshape(regions, CAP + 1, 1, HEAD),
+        "rep",
+        split_axis=0,
+        concat_axis=0,
+        tiled=True,
+        axis_index_groups=[seating(regions)],
     ).reshape(regions * (CAP + 1), HEAD)
     column, rows = kept_part(region_keep, residual)
     chosen = chosen_totals(got, column, rows)

time: 64.7 us -> 63.9 us (0.988)
  the two profiles are of different devices: /device:TPU:64 before, /device:TPU:2 now
where the time goes in v4:
time: 63.9 us; the launch traced here: 63.5 us
  waiting for transfers between devices  28.5 us (45%)
  starting transfers between devices  21.6 us (34%)
  Pallas kernels  10.1 us (16%)
  between operations  2.05 us (3%)
  local copies, waits for them, and re-layouts  0.69 us (1%)
    all_to_all x1, waiting for transfers between devices, body(): lax.all_to_all(sent.reshape(regions, CAP + 1, 1, HEAD), 'rep', split_axis...  23.4 us
    all_to_all x1, starting transfers between devices, body(): lax.all_to_all(sent.reshape(regions, CAP + 1, 1, HEAD), 'rep', split_axis...  14.5 us
    all_to_all x1, starting transfers between devices, body(): lax.all_to_all(chosen.reshape(pods, share, HEAD), 'outer', split_axis=0,...  7.1 us
    all_to_all x1, waiting for transfers between devices, body(): lax.all_to_all(chosen.reshape(pods, share, HEAD), 'outer', split_axis=0,...  5.12 us
    pallas_call x1, Pallas kernels, refreshed_slots(): pl.pallas_call(refresh_kernel, out_shape=jax.ShapeDtypeStruct((slots, HEA...  3.96 us
    pallas_call x1, Pallas kernels, send_rows(): pl.pallas_call(functools.partial(send_kernel, region_rows, band, BATCH),...  3.94 us
  transfers between devices with their start and end apart: 2, of which 2 were waited for; matrix products, arithmetic and copies ran while one was open for 1% of the time, Pallas kernels for 8%

profile of v4, /device:TPU:2, one launch (start us, length us, event | category | flops | bytes accessed | tf_op | source)
XLA Modules:
  0.0 63.5 jit_solution(12080937372459464961)
XLA Ops:
  0.6 3.9 %send_rows.1 = f32[2080,128]{1,0:T(8,128)} custom-call(s32[33]{0:T(128)} %bounds_hbm.1, s32[1,1024]{1,0:T(1,128)} %bitcast.17, bf16[128,8192]{1,0:T(8,128)(2,1)} %bitcast.15, bf16[128,1024]{1,0:T(8,128)(2,1)} %bitcast.16), custom_call_target="tpu_custom_call" | custom-call | flops 1000000000 | bytes 4194304 | tf_op jit(solution)/shard_map/send_rows/pallas_call | solution.py:161
  4.6 0.0 copy-start.2
  4.6 0.0 copy-start
  4.6 0.0 copy-start.1
  4.6 14.5 %all-to-all-start = ((f32[32,65,1,128]{3,2,1,0:T(1,128)}), f32[32,65,1,128]{3,2,1,0:T(1,128)S(1)}, u32[]{:S(2)}, u32[]{:S(2)}) async-start(f32[32,65,1,128]{3,2,1,0:T(1,128)} %bitcast.13), calls=%async_computation | async-start | bytes 2129920 | tf_op jit(solution)/shard_map/all_to_all | solution.py:322
  19.1 0.0 copy-done.2
  19.1 0.7 %fusion = (s32[1]{0:T(128)}, s32[1]{0:T(128)}) fusion(s32[33]{0:T(128)S(1)} %copy-done.2, s32[]{:T(128)S(6)} %select_n.7, s32[]{:T(128)S(6)} %select_n.6), kind=kLoop, calls=%fused_computation | loop fusion | bytes 24 | tf_op jit(solution)/shard_map/dynamic_slice | solution.py:319
  21.1 0.0 copy-done
  21.1 0.0 copy-done.1
  21.2 1.0 %kept_part.1 = (f32[256,128]{1,0:T(8,128)S(1)}, f32[256,128]{1,0:T(8,128)S(1)}) custom-call(s32[1,256]{1,0:T(1,128)S(1)} %copy-done.1, s32[1,256]{1,0:T(1,128)S(1)} %copy-done.1, f32[2304,128]{1,0:T(8,128)S(1)} %bitcast.11), custom_call_target="tpu_custom_call" | custom-call | flops 100000000 | bytes 4194304 | tf_op jit(solution)/shard_map/kept_part/pallas_call | solution.py:201
  22.1 23.4 %all-to-all-done = f32[32,65,1,128]{3,2,1,0:T(1,128)S(1)} async-done(((f32[32,65,1,128]{3,2,1,0:T(1,128)}), f32[32,65,1,128]{3,2,1,0:T(1,128)S(1)}, u32[]{:S(2)}, u32[]{:S(2)}) %all-to-all-start) | async-done | bytes 1064992 | tf_op jit(solution)/shard_map/all_to_all | solution.py:322
  45.5 1.2 %chosen_totals.1 = f32[256,128]{1,0:T(8,128)} custom-call(f32[2080,128]{1,0:T(8,128)S(1)} %bitcast.9, f32[256,128]{1,0:T(8,128)S(1)} %get-tuple-element.4.column_ref, f32[256,128]{1,0:T(8,128)S(1)} %get-tuple-element.5.rows_ref), custom_call_target="tpu_custom_call" | custom-call | flops 100000000 | bytes 4194304 | tf_op jit(solution)/shard_map/chosen_totals/pallas_call | solution.py:253
  46.7 7.1 %all-to-all-start.1 = ((f32[8,32,128]{2,1,0:T(8,128)}), f32[8,32,128]{2,1,0:T(8,128)S(1)}, u32[]{:S(2)}, u32[]{:S(2)}) async-start(f32[8,32,128]{2,1,0:T(8,128)} %bitcast.6), calls=%async_computation.1 | async-start | bytes 262144 | tf_op jit(solution)/shard_map/all_to_all | solution.py:333
  53.8 4.0 %refreshed_slots.1 = f32[2304,128]{1,0:T(8,128)} custom-call(s32[1]{0:T(128)S(6)} %sub.4.length_ref, f32[2080,128]{1,0:T(8,128)S(1)} %bitcast.10, s32[1,256]{1,0:T(1,128)S(1)} %copy-done.1, f32[2304,128]{1,0:T(8,128)S(1)} %bitcast.12), custom_call_target="tpu_custom_call" | custom-call | flops 3000000000 | bytes 4194304 | tf_op jit(solution)/shard_map/refreshed_slots/pallas_call | solution.py:291
  57.8 5.1 %all-to-all-done.1 = f32[8,32,128]{2,1,0:T(8,128)S(1)} async-done(((f32[8,32,128]{2,1,0:T(8,128)}), f32[8,32,128]{2,1,0:T(8,128)S(1)}, u32[]{:S(2)}, u32[]{:S(2)}) %all-to-all-start.1) | async-done | bytes 131104 | tf_op jit(solution)/shard_map/all_to_all | solution.py:333
  62.9 0.6 reduce_sum.9
Async XLA Ops:
  4.6 14.5 %copy-start.2 = (s32[33]{0:T(128)S(1)}, s32[33]{0:T(128)}, u32[]{:S(2)}) copy-start(s32[33]{0:T(128)} %bounds_hbm.1) | copy-start | bytes 400
  4.6 16.5 %copy-start = (f32[1,1,2304,128]{3,2,1,0:T(8,128)S(1)}, f32[1,1,2304,128]{3,2,1,0:T(8,128)}, u32[]{:S(2)}) copy-start(f32[1,1,2304,128]{3,2,1,0:T(8,128)} %param.11) | copy-start | bytes 3538948
  4.6 16.5 %copy-start.1 = (s32[1,256]{1,0:T(1,128)S(1)}, s32[1,256]{1,0:T(1,128)}, u32[]{:S(2)}) copy-start(s32[1,256]{1,0:T(1,128)} %keep_ref.3) | copy-start | bytes 3076
  4.6 40.9 %all-to-all-start = ((f32[32,65,1,128]{3,2,1,0:T(1,128)}), f32[32,65,1,128]{3,2,1,0:T(1,128)S(1)}, u32[]{:S(2)}, u32[]{:S(2)}) async-start(f32[32,65,1,128]{3,2,1,0:T(1,128)} %bitcast.13), calls=%async_computation | async-start | bytes 2129920 | tf_op jit(solution)/shard_map/all_to_all | solution.py:322
  46.7 16.2 %all-to-all-start.1 = ((f32[8,32,128]{2,1,0:T(8,128)}), f32[8,32,128]{2,1,0:T(8,128)S(1)}, u32[]{:S(2)}, u32[]{:S(2)}) async-start(f32[8,32,128]{2,1,0:T(8,128)} %bitcast.6), calls=%async_computation.1 | async-start | bytes 262144 | tf_op jit(solution)/shard_map/all_to_all | solution.py:333

commit v5 on v4

--- a/solution.py
+++ b/solution.py
@@ -327,11 +327,18 @@
         tiled=True,
         axis_index_groups=[seating(regions)],
     ).reshape(regions * (CAP + 1), HEAD)
-    column, rows = kept_part(region_keep, residual)
+    pod_seats = list(range(pods - 1, -1, -1))
+    seated_keep = region_keep.reshape(pods, -1)[::-1].reshape(region_keep.shape)
+    column, rows = kept_part(seated_keep, residual)
     chosen = chosen_totals(got, column, rows)
     share = chosen.shape[0] // pods
     shares = lax.all_to_all(
-        chosen.reshape(pods, share, HEAD), "outer", split_axis=0, concat_axis=0, tiled=True
+        chosen.reshape(pods, share, HEAD),
+        "outer",
+        split_axis=0,
+        concat_axis=0,
+        tiled=True,
+        axis_index_groups=[pod_seats],
     )
     merged = jnp.sum(shares, axis=0)
     refreshed = refreshed_slots(length, got, region_keep, residual, 3)

time: 63.9 us -> 61.7 us (0.966)
  the two profiles are of different devices: /device:TPU:2 before, /device:TPU:56 now
where the time goes in v5:
time: 61.7 us; the launch traced here: 61.3 us
  waiting for transfers between devices  27.3 us (44%)
  starting transfers between devices  19.4 us (31%)
  Pallas kernels  10.1 us (16%)
  between operations  1.96 us (3%)
  local copies, waits for them, and re-layouts  1.32 us (2%)
  other arithmetic  1.28 us (2%)
    all_to_all x1, waiting for transfers between devices, body(): lax.all_to_all(sent.reshape(regions, CAP + 1, 1, HEAD), 'rep', split_axis...  22.2 us
    all_to_all x1, starting transfers between devices, body(): lax.all_to_all(sent.reshape(regions, CAP + 1, 1, HEAD), 'rep', split_axis...  15.2 us
    all_to_all x1, waiting for transfers between devices, body(): lax.all_to_all(chosen.reshape(pods, share, HEAD), 'outer', split_axis=0,...  5.12 us
    all_to_all x1, starting transfers between devices, body(): lax.all_to_all(chosen.reshape(pods, share, HEAD), 'outer', split_axis=0,...  4.2 us
    pallas_call x1, Pallas kernels, refreshed_slots(): pl.pallas_call(refresh_kernel, out_shape=jax.ShapeDtypeStruct((slots, HEA...  3.96 us
    pallas_call x1, Pallas kernels, send_rows(): pl.pallas_call(functools.partial(send_kernel, region_rows, band, BATCH),...  3.94 us
  transfers between devices with their start and end apart: 2, of which 2 were waited for; matrix products, arithmetic and copies ran while one was open for 3% of the time, Pallas kernels for 8%

profile of v5, /device:TPU:56, one launch (start us, length us, event | category | flops | bytes accessed | tf_op | source)
XLA Modules:
  0.0 61.3 jit_solution(3208215132455257908)
XLA Ops:
  0.6 3.9 %send_rows.1 = f32[2080,128]{1,0:T(8,128)} custom-call(s32[33]{0:T(128)} %bounds_hbm.1, s32[1,1024]{1,0:T(1,128)} %bitcast.17, bf16[128,8192]{1,0:T(8,128)(2,1)} %bitcast.15, bf16[128,1024]{1,0:T(8,128)(2,1)} %bitcast.16), custom_call_target="tpu_custom_call" | custom-call | flops 1000000000 | bytes 4194304 | tf_op jit(solution)/shard_map/send_rows/pallas_call | solution.py:161
  4.6 0.0 copy-start.1
  4.6 0.0 copy-start.2
  4.6 0.0 copy-start
  4.6 15.2 %all-to-all-start = ((f32[32,65,1,128]{3,2,1,0:T(1,128)}), f32[32,65,1,128]{3,2,1,0:T(1,128)S(1)}, u32[]{:S(2)}, u32[]{:S(2)}) async-start(f32[32,65,1,128]{3,2,1,0:T(1,128)} %bitcast.13), calls=%async_computation | async-start | bytes 2129920 | tf_op jit(solution)/shard_map/all_to_all | solution.py:322
  19.8 0.5 broadcast.3
  20.3 0.0 copy-done.1
  20.3 0.7 %reduce.3 = s32[256]{0:T(256)S(1)} reduce(s32[1,256]{1,0:T(1,128)S(1)} %copy-done.1, s32[]{:T(128)} %broadcast.3), dimensions={0}, to_apply=%param.10.reduce_sub_computation.3 | reduce | bytes 2052 | tf_op args[4]
  21.0 0.1 reshape.28
  21.1 0.1 reshape.29.slots_ref.keep_ref
  21.1 0.0 copy-done.2
  21.1 0.6 %fusion = (s32[1]{0:T(128)}, s32[1]{0:T(128)}) fusion(s32[33]{0:T(128)S(1)} %copy-done.2, s32[]{:T(128)S(6)} %select_n.7, s32[]{:T(128)S(6)} %select_n.6), kind=kLoop, calls=%fused_computation | loop fusion | bytes 24 | tf_op jit(solution)/shard_map/dynamic_slice | solution.py:319
  23.0 0.0 copy-done
  23.0 1.0 %kept_part.1 = (f32[256,128]{1,0:T(8,128)S(1)}, f32[256,128]{1,0:T(8,128)S(1)}) custom-call(s32[1,256]{1,0:T(1,128)S(1)} %reshape.29.slots_ref.keep_ref, s32[1,256]{1,0:T(1,128)S(1)} %reshape.29.slots_ref.keep_ref, f32[2304,128]{1,0:T(8,128)S(1)} %bitcast.11), custom_call_target="tpu_custom_call" | custom-call | flops 100000000 | bytes 4194304 | tf_op jit(solution)/shard_map/kept_part/pallas_call | solution.py:201
  24.0 22.2 %all-to-all-done = f32[32,65,1,128]{3,2,1,0:T(1,128)S(1)} async-done(((f32[32,65,1,128]{3,2,1,0:T(1,128)}), f32[32,65,1,128]{3,2,1,0:T(1,128)S(1)}, u32[]{:S(2)}, u32[]{:S(2)}) %all-to-all-start) | async-done | bytes 1064992 | tf_op jit(solution)/shard_map/all_to_all | solution.py:322
  46.2 1.2 %chosen_totals.1 = f32[256,128]{1,0:T(8,128)} custom-call(f32[2080,128]{1,0:T(8,128)S(1)} %bitcast.9, f32[256,128]{1,0:T(8,128)S(1)} %get-tuple-element.4.column_ref, f32[256,128]{1,0:T(8,128)S(1)} %get-tuple-element.5.rows_ref), custom_call_target="tpu_custom_call" | custom-call | flops 100000000 | bytes 4194304 | tf_op jit(solution)/shard_map/chosen_totals/pallas_call | solution.py:253
  47.4 4.2 %all-to-all-start.1 = ((f32[8,32,128]{2,1,0:T(8,128)}), f32[8,32,128]{2,1,0:T(8,128)S(1)}, u32[]{:S(2)}, u32[]{:S(2)}) async-start(f32[8,32,128]{2,1,0:T(8,128)} %bitcast.6), calls=%async_computation.1 | async-start | bytes 262144 | tf_op jit(solution)/shard_map/all_to_all | solution.py:335
  51.6 4.0 %refreshed_slots.1 = f32[2304,128]{1,0:T(8,128)} custom-call(s32[1]{0:T(128)S(6)} %sub.4.length_ref, f32[2080,128]{1,0:T(8,128)S(1)} %bitcast.10, s32[1,256]{1,0:T(1,128)S(1)} %copy-done.1, f32[2304,128]{1,0:T(8,128)S(1)} %bitcast.12), custom_call_target="tpu_custom_call" | custom-call | flops 3000000000 | bytes 4194304 | tf_op jit(solution)/shard_map/refreshed_slots/pallas_call | solution.py:291
  55.6 5.1 %all-to-all-done.1 = f32[8,32,128]{2,1,0:T(8,128)S(1)} async-done(((f32[8,32,128]{2,1,0:T(8,128)}), f32[8,32,128]{2,1,0:T(8,128)S(1)}, u32[]{:S(2)}, u32[]{:S(2)}) %all-to-all-start.1) | async-done | bytes 131104 | tf_op jit(solution)/shard_map/all_to_all | solution.py:335
  60.7 0.6 %reduce_sum.9 = f32[32,128]{1,0:T(8,128)} reduce(f32[8,32,128]{2,1,0:T(8,128)S(1)} %all-to-all-done.1, f32[]{:T(128)} %constant.3.clone.1), dimensions={0}, to_apply=%region_0.0 | reduce | flops 28672 | bytes 147460 | tf_op jit(solution)/shard_map/reduce_sum | solution.py:343
  (1 shorter events, 0.0 us)
Async XLA Ops:
  4.6 15.7 %copy-start.1 = (s32[1,256]{1,0:T(1,128)S(1)}, s32[1,256]{1,0:T(1,128)}, u32[]{:S(2)}) copy-start(s32[1,256]{1,0:T(1,128)} %keep_ref.1) | copy-start | bytes 3076
  4.6 16.6 %copy-start.2 = (s32[33]{0:T(128)S(1)}, s32[33]{0:T(128)}, u32[]{:S(2)}) copy-start(s32[33]{0:T(128)} %bounds_hbm.1) | copy-start | bytes 400
  4.6 18.4 %copy-start = (f32[1,1,2304,128]{3,2,1,0:T(8,128)S(1)}, f32[1,1,2304,128]{3,2,1,0:T(8,128)}, u32[]{:S(2)}) copy-start(f32[1,1,2304,128]{3,2,1,0:T(8,128)} %param.11) | copy-start | bytes 3538948
  4.6 41.6 %all-to-all-start = ((f32[32,65,1,128]{3,2,1,0:T(1,128)}), f32[32,65,1,128]{3,2,1,0:T(1,128)S(1)}, u32[]{:S(2)}, u32[]{:S(2)}) async-start(f32[32,65,1,128]{3,2,1,0:T(1,128)} %bitcast.13), calls=%async_computation | async-start | bytes 2129920 | tf_op jit(solution)/shard_map/all_to_all | solution.py:322
  47.4 13.3 %all-to-all-start.1 = ((f32[8,32,128]{2,1,0:T(8,128)}), f32[8,32,128]{2,1,0:T(8,128)S(1)}, u32[]{:S(2)}, u32[]{:S(2)}) async-start(f32[8,32,128]{2,1,0:T(8,128)} %bitcast.6), calls=%async_computation.1 | async-start | bytes 262144 | tf_op jit(solution)/shard_map/all_to_all | solution.py:335

commit v6 on v5

--- a/solution.py
+++ b/solution.py
@@ -21,7 +21,7 @@
 
 
 def seating(regions):
-    return [regions - 1 - seat for seat in range(regions)]
+    return [seat ^ (regions - BATCH) for seat in range(regions)]
 
 
 def send_kernel(

time: 61.7 us -> 61 us (0.989)
  starting transfers between devices: 19.4 us -> 18.5 us
    all_to_all x1, starting transfers between devices: 15.2 us -> 14.3 us  [body(): lax.all_to_all(sent.reshape(regions, CAP + 1, 1, HEAD), 'rep', split_axis...]
where the time goes in v6:
time: 61 us; the launch traced here: 60.7 us
  waiting for transfers between devices  27.6 us (45%)
  starting transfers between devices  18.5 us (30%)
  Pallas kernels  10.1 us (17%)
  between operations  1.96 us (3%)
  local copies, waits for them, and re-layouts  1.32 us (2%)
  other arithmetic  1.28 us (2%)
    all_to_all x1, waiting for transfers between devices, body(): lax.all_to_all(sent.reshape(regions, CAP + 1, 1, HEAD), 'rep', split_axis...  22.5 us
    all_to_all x1, starting transfers between devices, body(): lax.all_to_all(sent.reshape(regions, CAP + 1, 1, HEAD), 'rep', split_axis...  14.3 us
    all_to_all x1, waiting for transfers between devices, body(): lax.all_to_all(chosen.reshape(pods, share, HEAD), 'outer', split_axis=0,...  5.12 us
    all_to_all x1, starting transfers between devices, body(): lax.all_to_all(chosen.reshape(pods, share, HEAD), 'outer', split_axis=0,...  4.19 us
    pallas_call x1, Pallas kernels, refreshed_slots(): pl.pallas_call(refresh_kernel, out_shape=jax.ShapeDtypeStruct((slots, HEA...  3.96 us
    pallas_call x1, Pallas kernels, send_rows(): pl.pallas_call(functools.partial(send_kernel, region_rows, band, BATCH),...  3.94 us
  transfers between devices with their start and end apart: 2, of which 2 were waited for; matrix products, arithmetic and copies ran while one was open for 3% of the time, Pallas kernels for 8%

profile of v6, /device:TPU:56, one launch (start us, length us, event | category | flops | bytes accessed | tf_op | source)
XLA Modules:
  0.0 60.7 jit_solution(8286533896884450078)
XLA Ops:
  0.6 3.9 %send_rows.1 = f32[2080,128]{1,0:T(8,128)} custom-call(s32[33]{0:T(128)} %bounds_hbm.1, s32[1,1024]{1,0:T(1,128)} %bitcast.17, bf16[128,8192]{1,0:T(8,128)(2,1)} %bitcast.15, bf16[128,1024]{1,0:T(8,128)(2,1)} %bitcast.16), custom_call_target="tpu_custom_call" | custom-call | flops 1000000000 | bytes 4194304 | tf_op jit(solution)/shard_map/send_rows/pallas_call | solution.py:161
  4.6 0.0 copy-start.1
  4.6 0.0 copy-start.2
  4.6 0.0 copy-start
  4.6 14.3 %all-to-all-start = ((f32[32,65,1,128]{3,2,1,0:T(1,128)}), f32[32,65,1,128]{3,2,1,0:T(1,128)S(1)}, u32[]{:S(2)}, u32[]{:S(2)}) async-start(f32[32,65,1,128]{3,2,1,0:T(1,128)} %bitcast.13), calls=%async_computation | async-start | bytes 2129920 | tf_op jit(solution)/shard_map/all_to_all | solution.py:322
  18.9 0.5 broadcast.3
  19.4 0.0 copy-done.1
  19.4 0.7 %reduce.3 = s32[256]{0:T(256)S(1)} reduce(s32[1,256]{1,0:T(1,128)S(1)} %copy-done.1, s32[]{:T(128)} %broadcast.3), dimensions={0}, to_apply=%param.10.reduce_sub_computation.3 | reduce | bytes 2052 | tf_op args[4]
  20.1 0.1 reshape.28
  20.2 0.1 reshape.29.slots_ref.keep_ref
  20.2 0.0 copy-done.2
  20.2 0.6 %fusion = (s32[1]{0:T(128)}, s32[1]{0:T(128)}) fusion(s32[33]{0:T(128)S(1)} %copy-done.2, s32[]{:T(128)S(6)} %select_n.7, s32[]{:T(128)S(6)} %select_n.6), kind=kLoop, calls=%fused_computation | loop fusion | bytes 24 | tf_op jit(solution)/shard_map/dynamic_slice | solution.py:319
  22.1 0.0 copy-done
  22.1 1.0 %kept_part.1 = (f32[256,128]{1,0:T(8,128)S(1)}, f32[256,128]{1,0:T(8,128)S(1)}) custom-call(s32[1,256]{1,0:T(1,128)S(1)} %reshape.29.slots_ref.keep_ref, s32[1,256]{1,0:T(1,128)S(1)} %reshape.29.slots_ref.keep_ref, f32[2304,128]{1,0:T(8,128)S(1)} %bitcast.11), custom_call_target="tpu_custom_call" | custom-call | flops 100000000 | bytes 4194304 | tf_op jit(solution)/shard_map/kept_part/pallas_call | solution.py:201
  23.1 22.5 %all-to-all-done = f32[32,65,1,128]{3,2,1,0:T(1,128)S(1)} async-done(((f32[32,65,1,128]{3,2,1,0:T(1,128)}), f32[32,65,1,128]{3,2,1,0:T(1,128)S(1)}, u32[]{:S(2)}, u32[]{:S(2)}) %all-to-all-start) | async-done | bytes 1064992 | tf_op jit(solution)/shard_map/all_to_all | solution.py:322
  45.6 1.2 %chosen_totals.1 = f32[256,128]{1,0:T(8,128)} custom-call(f32[2080,128]{1,0:T(8,128)S(1)} %bitcast.9, f32[256,128]{1,0:T(8,128)S(1)} %get-tuple-element.4.column_ref, f32[256,128]{1,0:T(8,128)S(1)} %get-tuple-element.5.rows_ref), custom_call_target="tpu_custom_call" | custom-call | flops 100000000 | bytes 4194304 | tf_op jit(solution)/shard_map/chosen_totals/pallas_call | solution.py:253
  46.8 4.2 %all-to-all-start.1 = ((f32[8,32,128]{2,1,0:T(8,128)}), f32[8,32,128]{2,1,0:T(8,128)S(1)}, u32[]{:S(2)}, u32[]{:S(2)}) async-start(f32[8,32,128]{2,1,0:T(8,128)} %bitcast.6), calls=%async_computation.1 | async-start | bytes 262144 | tf_op jit(solution)/shard_map/all_to_all | solution.py:335
  51.0 4.0 %refreshed_slots.1 = f32[2304,128]{1,0:T(8,128)} custom-call(s32[1]{0:T(128)S(6)} %sub.4.length_ref, f32[2080,128]{1,0:T(8,128)S(1)} %bitcast.10, s32[1,256]{1,0:T(1,128)S(1)} %copy-done.1, f32[2304,128]{1,0:T(8,128)S(1)} %bitcast.12), custom_call_target="tpu_custom_call" | custom-call | flops 3000000000 | bytes 4194304 | tf_op jit(solution)/shard_map/refreshed_slots/pallas_call | solution.py:291
  55.0 5.1 %all-to-all-done.1 = f32[8,32,128]{2,1,0:T(8,128)S(1)} async-done(((f32[8,32,128]{2,1,0:T(8,128)}), f32[8,32,128]{2,1,0:T(8,128)S(1)}, u32[]{:S(2)}, u32[]{:S(2)}) %all-to-all-start.1) | async-done | bytes 131104 | tf_op jit(solution)/shard_map/all_to_all | solution.py:335
  60.1 0.6 %reduce_sum.9 = f32[32,128]{1,0:T(8,128)} reduce(f32[8,32,128]{2,1,0:T(8,128)S(1)} %all-to-all-done.1, f32[]{:T(128)} %constant.3.clone.1), dimensions={0}, to_apply=%region_0.0 | reduce | flops 28672 | bytes 147460 | tf_op jit(solution)/shard_map/reduce_sum | solution.py:343
  (1 shorter events, 0.0 us)
Async XLA Ops:
  4.6 14.8 %copy-start.1 = (s32[1,256]{1,0:T(1,128)S(1)}, s32[1,256]{1,0:T(1,128)}, u32[]{:S(2)}) copy-start(s32[1,256]{1,0:T(1,128)} %keep_ref.1) | copy-start | bytes 3076
  4.6 15.6 %copy-start.2 = (s32[33]{0:T(128)S(1)}, s32[33]{0:T(128)}, u32[]{:S(2)}) copy-start(s32[33]{0:T(128)} %bounds_hbm.1) | copy-start | bytes 400
  4.6 17.5 %copy-start = (f32[1,1,2304,128]{3,2,1,0:T(8,128)S(1)}, f32[1,1,2304,128]{3,2,1,0:T(8,128)}, u32[]{:S(2)}) copy-start(f32[1,1,2304,128]{3,2,1,0:T(8,128)} %param.11) | copy-start | bytes 3538948
  4.6 41.0 %all-to-all-start = ((f32[32,65,1,128]{3,2,1,0:T(1,128)}), f32[32,65,1,128]{3,2,1,0:T(1,128)S(1)}, u32[]{:S(2)}, u32[]{:S(2)}) async-start(f32[32,65,1,128]{3,2,1,0:T(1,128)} %bitcast.13), calls=%async_computation | async-start | bytes 2129920 | tf_op jit(solution)/shard_map/all_to_all | solution.py:322
  46.8 13.3 %all-to-all-start.1 = ((f32[8,32,128]{2,1,0:T(8,128)}), f32[8,32,128]{2,1,0:T(8,128)S(1)}, u32[]{:S(2)}, u32[]{:S(2)}) async-start(f32[8,32,128]{2,1,0:T(8,128)} %bitcast.6), calls=%async_computation.1 | async-start | bytes 262144 | tf_op jit(solution)/shard_map/all_to_all | solution.py:335
